TPU v7x, 32 devices: a whole 2x2x4 slice. The times are simulated.
32 devices in a mesh: dp: 8 (over y, x, core), seq: 4 (over z).
Axes of the slice: x: 2, y: 2, z: 4, core: 2. Of those that a mesh axis runs over, the one named last changes fastest.
Arguments:
- tokens: bfloat16 [32, 1024, 512], P('dp', 'seq'), may hold values from -6 to 6
- memory: bfloat16 [32, 256, 512], P('dp', 'seq'), may hold values from -6 to 6
- doc_lengths: int32 [32, 32], P('dp'), may hold values from 0 to 1024, as said below
- src_lengths: int32 [32, 32], P('dp'), may hold values from 1 to 225, as said below
- cotangent: bfloat16 [32, 1024, 512], P('dp', 'seq'), may hold values from -6 to 6
- w_qkv: bfloat16 [512, 1536], replicated, may hold values from -0.25 to 0.25
- qv_bias: bfloat16 [1024], replicated, may hold values from -1.75 to 1.75
- self_out: bfloat16 [512, 512], replicated, may hold values from -0.75 to 0.75
- self_out_bias: bfloat16 [512], replicated, may hold values from -1.75 to 1.75
- cross_query: bfloat16 [512, 512], replicated, may hold values from -0.25 to 0.25
- cross_q_bias: bfloat16 [512], replicated, may hold values from -1.75 to 1.75
- cross_kv: bfloat16 [512, 1024], replicated, may hold values from -0.25 to 0.25
- cross_v_bias: bfloat16 [512], replicated, may hold values from -1.75 to 1.75
- cross_out: bfloat16 [512, 512], replicated, may hold values from -0.75 to 0.75
- cross_out_bias: bfloat16 [512], replicated, may hold values from -1.75 to 1.75
- ffn_in: bfloat16 [512, 2048], replicated, may hold values from -0.25 to 0.25
- ffn_in_bias: bfloat16 [2048], replicated, may hold values from -1.75 to 1.75
- ffn_out: bfloat16 [2048, 512], replicated, may hold values from -0.1875 to 0.1875
- ffn_out_bias: bfloat16 [512], replicated, may hold values from -1.75 to 1.75
- norm_gains: bfloat16 [3, 512], replicated, may hold values from 0.5 to 1.5
- norm_biases: bfloat16 [3, 512], replicated, may hold values from -1.75 to 1.75
Outputs:
- output: bfloat16 [32, 1024, 512], P('dp', 'seq')
- d_tokens: float32 [32, 1024, 512], P('dp', 'seq')
- d_memory: float32 [32, 256, 512], P('dp', 'seq')
- d_w_qkv: float32 [512, 1536], replicated
- d_qv_bias: float32 [1024], replicated
- d_self_out: float32 [512, 512], replicated
- d_self_out_bias: float32 [512], replicated
- d_cross_query: float32 [512, 512], replicated
- d_cross_q_bias: float32 [512], replicated
- d_cross_kv: float32 [512, 1024], replicated
- d_cross_v_bias: float32 [512], replicated
- d_cross_out: float32 [512, 512], replicated
- d_cross_out_bias: float32 [512], replicated
- d_ffn_in: float32 [512, 2048], replicated
- d_ffn_in_bias: float32 [2048], replicated
- d_ffn_out: float32 [2048, 512], replicated
- d_ffn_out_bias: float32 [512], replicated
- d_norm_gains: float32 [3, 512], replicated
- d_norm_biases: float32 [3, 512], replicated
Inputs may be any that keep to these rules, and one draw needn't show every extreme that they name: `doc_lengths`: the 32 lengths of a row sum to at most 1024; positions after their sum are padding. Document j of a target row belongs with document j of its source row. `src_lengths`: the 32 lengths of a row sum to 256.
All inputs are finite; a program needn't handle non-finite values.
Results may differ from a plain program's by a relative error of at most 0.018.
Values may be sent and summed in bfloat16 or wider, within the bound.
A program may use at most 256 MiB of HBM per device.

v0:
```python
import functools
import jax
import jax.numpy as jnp
from jax import lax
from jax.experimental import pallas as pl
from jax.experimental.pallas import tpu as pltpu
from jax.sharding import PartitionSpec as P

HEADS = 8
HEAD = 64
NDOC = 32
AUG = HEAD + 16
MASKED = -1e9
LOG2E = 1.4426950408889634
SCALE = HEAD**-0.5
F32 = jnp.float32
BF16 = jnp.bfloat16
TB = 256

V_Q, V_V, V_SO, V_CQ, V_CV, V_CO, V_FI, V_FO, V_G, V_B = 0, 1, 2, 3, 4, 5, 6, 10, 11, 14
VECS = 24
G_IN, G_OUT, G_CO, G_CQ, G_CK, G_SO, G_QKV = 0, 4, 8, 9, 10, 12, 13
STREAMS = ((G_OUT, 4), (G_IN, 4), (G_CO, 5), (G_QKV, 3))
STEPS = 8
COPIES = (1, 2, 2, 6, 6, 2, 2, 1)
OWN = sum(COPIES)


def vec_of(ref, start, length):
    return ref[start : start + length].astype(F32).reshape(1, length)


def mm(left, right, lc=1, rc=0):
    return lax.dot_general(
        left, right, (((lc,), (rc,)), ((), ())), preferred_element_type=F32
    )


def row_ids(lengths, row, size):
    rows, docs = lengths.shape
    at_row = lax.broadcasted_iota(jnp.int32, (rows, docs), 0) == row
    own = jnp.sum(jnp.where(at_row, lengths.astype(F32), 0.0), axis=0, keepdims=True)
    own = jnp.broadcast_to(own, (docs, docs))
    down = lax.broadcasted_iota(jnp.int32, (docs, docs), 0)
    over = lax.broadcasted_iota(jnp.int32, (docs, docs), 1)
    ends_col = jnp.sum(jnp.where(over <= down, own, 0.0), axis=1, keepdims=True)
    own_col = jnp.sum(jnp.where(over == down, own, 0.0), axis=1, keepdims=True)
    ends_row = jnp.sum(
        jnp.where(down <= over, jnp.broadcast_to(own_col, (docs, docs)), 0.0),
        axis=0,
        keepdims=True,
    )
    place_row = lax.broadcasted_iota(jnp.int32, (docs, size), 1).astype(F32)
    place_col = lax.broadcasted_iota(jnp.int32, (size, docs), 0).astype(F32)
    ids_row = jnp.sum(jnp.where(ends_col <= place_row, 1.0, 0.0), axis=0, keepdims=True)
    ids_col = jnp.sum(jnp.where(ends_row <= place_col, 1.0, 0.0), axis=1, keepdims=True)
    return ids_row, ids_col


def self_mask(mask_ref, lengths, row, size):
    ids_row, ids_col = row_ids(lengths, row, size)
    for kb in range(size // TB):
        for qb in range(kb, size // TB):
            ks, qs = slice(kb * TB, (kb + 1) * TB), slice(qb * TB, (qb + 1) * TB)
            seen = ids_col[ks] == ids_row[:, qs]
            if kb == qb:
                down = lax.broadcasted_iota(jnp.int32, (TB, TB), 0)
                over = lax.broadcasted_iota(jnp.int32, (TB, TB), 1)
                seen = seen & (down <= over)
            mask_ref[ks, qs] = jnp.where(seen, 0.0, MASKED)


def cross_mask(mask_ref, lengths, src_lengths, row, size, src):
    ids_row, _ = row_ids(lengths, row, size)
    _, src_col = row_ids(src_lengths, row, src)
    for qb in range(size // TB):
        qs = slice(qb * TB, (qb + 1) * TB)
        seen = (src_col == ids_row[:, qs]) | (ids_row[:, qs] == float(NDOC))
        mask_ref[:, qs] = jnp.where(seen, 0.0, MASKED)


def half_of(values, half):
    down = lax.broadcasted_iota(jnp.int32, values.shape, 0)
    keep = (down >= HEAD) if half else (down < HEAD)
    return jnp.where(keep, values, jnp.zeros_like(values))


def normalize(h):
    center = h - jnp.mean(h, axis=-1, keepdims=True)
    spread = jnp.mean(center * center, axis=-1, keepdims=True)
    rstd = lax.rsqrt(spread + 1e-05)
    return center * rstd, rstd


def norm_back(grad, xh, rstd, gain):
    gs = grad * gain
    m1 = jnp.mean(gs, axis=-1, keepdims=True)
    m2 = jnp.mean(gs * xh, axis=-1, keepdims=True)
    dh = (gs - m1 - xh * m2) * rstd
    return (
        dh,
        jnp.sum(grad * xh, axis=0, keepdims=True),
        jnp.sum(grad, axis=0, keepdims=True),
    )


def row_attend(k_ref, qt_ref, vt_ref, mask_ref, ctx_ref, lse_ref, size, key_end):
    @pl.loop(0, HEADS // 2)
    def _(pair):
        lanes = pl.ds(pl.multiple_of(pair * 2 * HEAD, 2 * HEAD), 2 * HEAD)
        for half in range(2):
            head = pair * 2 + half
            for qb in range(size // TB):
                ke, qs = key_end(qb), slice(qb * TB, (qb + 1) * TB)
                s = mm(k_ref[0:ke, lanes], half_of(qt_ref[lanes, qs], half))
                s = s + mask_ref[0:ke, qs]
                m = jnp.max(s, axis=0, keepdims=True)
                p = jnp.exp2(s - m).astype(BF16)
                o = mm(vt_ref[pl.ds(pl.multiple_of(head * AUG, 16), AUG), 0:ke], p)
                total = o[HEAD : HEAD + 1]
                ctx_ref[pl.ds(pl.multiple_of(head * HEAD, HEAD), HEAD), qs] = (
                    o[:HEAD] * (1.0 / total)
                ).astype(BF16)
                lse_ref[head, :, qs] = m + jnp.log2(total)


class Mover:
    def __init__(self, sems):
        self.sems, self.used, self.pending = sems, 0, {}

    def start(self, name, src, dst):
        copy = pltpu.make_async_copy(src, dst, self.sems.at[self.used])
        self.used += 1
        copy.start()
        self.pending[name] = copy

    def wait(self, *names):
        for name in names:
            self.pending.pop(name).wait()

    def finish(self):
        self.wait(*list(self.pending))


def meet(peers):
    barrier = pltpu.get_barrier_semaphore()
    for peer in peers:
        pl.semaphore_signal(barrier, inc=1, device_id=peer, device_id_type=pl.DeviceIdType.MESH)
    pl.semaphore_wait(barrier, len(peers))


def remote(src, dst, sends, recvs, index, peer):
    return pltpu.make_async_remote_copy(
        src_ref=src, dst_ref=dst, send_sem=sends.at[index], recv_sem=recvs.at[index],
        device_id=peer, device_id_type=pl.DeviceIdType.MESH,
    )


FWD_OUTS = 22


def forward_kernel(
    tok_ref, src_ref, cot_ref, tl_ref, sl_ref, bqv, bso, bcq, bcv, bco, gains, shifts,
    wqkv_h, wso_h, wcq_h, wckv_h, wco_h, *rest,
):
    outs, rest = rest[:FWD_OUTS], rest[FWD_OUTS:]
    cot_out = outs[0]
    kept, rest = rest[: FWD_OUTS - 1], rest[FWD_OUTS - 1 :]
    (wqkv_ref, wso_ref, wcq_ref, wckv_ref, wco_ref, mask, mask2, vt, v2t, y1,
     sems, sends, recvs) = rest
    (x_ref, mem_ref, q_ref, qt_ref, k_ref, kt_ref, v_ref, ctx_ref, lse_ref, xh1_ref, rs1_ref,
     q2_ref, q2t_ref, k2_ref, k2t_ref, v2_ref, c2_ref, lse2_ref, y2_ref, xh2_ref, rs2_ref) = kept
    size, width = x_ref.shape
    src = mem_ref.shape[0]
    seq = tok_ref.shape[0]
    blocks = size // TB
    row = lax.axis_index("seq")
    mover = Mover(sems)
    mover.start("wqkv", wqkv_h, wqkv_ref)
    mover.start("wckv", wckv_h, wckv_ref)
    mover.start("wso", wso_h, wso_ref)
    mover.start("wcq", wcq_h, wcq_ref)
    mover.start("wco", wco_h, wco_ref)

    def place(block, length):
        return pl.ds(pl.multiple_of(block * length, length), length)

    peers = [{"seq": lax.rem(row + d, seq)} for d in range(1, seq)]
    meet(peers)

    def exchange(source, target, length, kind):
        copies = []
        for d in range(1, seq):
            to = lax.rem(row + d, seq)
            copy = remote(source.at[to], target.at[place(row, length)], sends, recvs, kind * seq + d, {"seq": to})
            copy.start()
            copies.append(copy)
        mover.start((kind, "own"), source.at[row], target.at[place(row, length)])
        return copies

    tok_copies = exchange(tok_ref, x_ref, TB, 0)
    mem_copies = exchange(src_ref, mem_ref, src // seq, 1)

    for head in range(HEADS):
        vt[head * AUG + HEAD : (head + 1) * AUG, :] = jnp.ones((AUG - HEAD, size), BF16)
        v2t[head * AUG + HEAD : (head + 1) * AUG, :] = jnp.ones((AUG - HEAD, src), BF16)
    self_mask(mask, tl_ref[...], row, size)
    cross_mask(mask2, tl_ref[...], sl_ref[...], row, size, src)

    def put_vt(ref, values, place):
        for head in range(HEADS):
            ref[head * AUG : head * AUG + HEAD, place] = values[head * HEAD : (head + 1) * HEAD]

    mover.wait("wqkv", (0, "own"))
    for d in range(seq):
        if d:
            tok_copies[d - 1].wait_recv()
        ts = place(lax.rem(row + seq - d, seq), TB)
        xb = x_ref[ts, :]
        q = ((mm(xb, wqkv_ref[:, :width]) + vec_of(bqv, 0, width)) * (SCALE * LOG2E)).astype(BF16)
        q_ref[ts, :] = q
        qt_ref[:, ts] = q.T
        k = mm(xb, wqkv_ref[:, width : 2 * width]).astype(BF16)
        k_ref[ts, :] = k
        kt_ref[:, ts] = k.T
        v = (mm(xb, wqkv_ref[:, 2 * width :]) + vec_of(bqv, width, width)).astype(BF16)
        v_ref[ts, :] = v
        put_vt(vt, v.T, ts)
    mover.wait("wckv", (1, "own"))
    for copy in mem_copies:
        copy.wait_recv()
    cot_copies = exchange(cot_ref, cot_out, TB, 2)
    for i in (0, 1, 2, 3, 4, 5, 6):
        mover.start(i, kept[i], outs[1 + i])
    k2 = mm(mem_ref[...], wckv_ref[:, :width]).astype(BF16)
    k2_ref[...] = k2
    k2t_ref[...] = k2.T
    v2 = (mm(mem_ref[...], wckv_ref[:, width:]) + vec_of(bcv, 0, width)).astype(BF16)
    v2_ref[...] = v2
    put_vt(v2t, v2.T, slice(None))
    for i in (13, 14, 15):
        mover.start(i, kept[i], outs[1 + i])

    row_attend(k_ref, qt_ref, vt, mask, ctx_ref, lse_ref, size, lambda qb: (qb + 1) * TB)
    for i in (7, 8):
        mover.start(i, kept[i], outs[1 + i])
    mover.wait("wso", "wcq")
    for tb in range(blocks):
        ts = slice(tb * TB, (tb + 1) * TB)
        h1 = x_ref[ts, :].astype(F32) + mm(ctx_ref[:, ts].T, wso_ref[...]) + vec_of(bso, 0, width)
        xh, rstd = normalize(h1)
        xh1_ref[ts, :] = xh.astype(BF16)
        rs1_ref[ts, :] = rstd
        yb = xh * gains[0:1, :].astype(F32) + shifts[0:1, :].astype(F32)
        y1[ts, :] = yb
        q2 = ((mm(yb.astype(BF16), wcq_ref[...]) + vec_of(bcq, 0, width)) * (SCALE * LOG2E)).astype(BF16)
        q2_ref[ts, :] = q2
        q2t_ref[:, ts] = q2.T
    for i in (9, 10, 11, 12):
        mover.start(i, kept[i], outs[1 + i])
    row_attend(k2_ref, q2t_ref, v2t, mask2, c2_ref, lse2_ref, size, lambda qb: src)
    for i in (16, 17):
        mover.start(i, kept[i], outs[1 + i])
    mover.wait("wco")
    for tb in range(blocks):
        ts = slice(tb * TB, (tb + 1) * TB)
        h2 = y1[ts, :] + mm(c2_ref[:, ts].T, wco_ref[...]) + vec_of(bco, 0, width)
        xh, rstd = normalize(h2)
        xh2_ref[ts, :] = xh.astype(BF16)
        rs2_ref[ts, :] = rstd
        y2_ref[ts, :] = xh * gains[1:2, :].astype(F32) + shifts[1:2, :].astype(F32)
        for i in (18, 19, 20):
            mover.start((i, tb), kept[i].at[ts], outs[1 + i].at[ts])
    for copy in cot_copies:
        copy.wait_recv()
    for copy in tok_copies + mem_copies + cot_copies:
        copy.wait_send()
    mover.finish()


def put_halves(ref, rows, values):
    half = values.shape[1] // 2
    ref[0, rows, :] = values[:, :half].astype(BF16)
    ref[1, rows, :] = values[:, half:].astype(BF16)


def ffn_kernel(
    y2_h, xh2_h, rs2_h, cot_h, bfi, bfo, gains, shifts, win_h, wout_h,
    out_h, dh2_h, dw_h, dvec_ref,
    y2_ref, xh2_ref, rs2_ref, cot_ref, win_ref, wout_ref, out_ref, dh2_ref, dw_ref,
    a_s, du_s, slope_s, y2b_s, dz_s, sems,
):
    size, width = y2_ref.shape
    inner = win_ref.shape[1]
    cols = [slice(j, j + width) for j in range(0, inner, width)]
    mover = Mover(sems)
    for name, src, dst in (
        ("y2", y2_h, y2_ref), ("win", win_h, win_ref), ("wout", wout_h, wout_ref),
        ("cot", cot_h, cot_ref), ("xh2", xh2_h, xh2_ref), ("rs2", rs2_h, rs2_ref),
    ):
        mover.start(name, src, dst)
    gain2, shift2, gain1 = gains[2:3, :].astype(F32), shifts[2:3, :].astype(F32), gains[1:2, :].astype(F32)
    dvec_ref[...] = jnp.zeros_like(dvec_ref)
    mover.wait("y2", "win", "wout", "cot", "xh2", "rs2")

    @pl.loop(0, size // TB)
    def _(tb):
        ts = pl.ds(pl.multiple_of(tb * TB, TB), TB)
        y2 = y2_ref[ts, :]
        y2b = y2.astype(BF16)
        y2b_s[ts, :] = y2b
        h3 = y2 + vec_of(bfo, 0, width)
        for j, cs in enumerate(cols):
            u = mm(y2b, win_ref[:, cs]) + vec_of(bfi, j * width, width)
            sg = 0.5 * jnp.tanh(0.5 * u) + 0.5
            act = u * sg
            slope_s[:, cs] = sg + act * (1.0 - sg)
            act = act.astype(BF16)
            a_s[ts, cs] = act
            h3 = h3 + mm(act, wout_ref[cs, :])
        xh, rstd = normalize(h3)
        out_ref[ts, :] = (xh * gain2 + shift2).astype(BF16)
        grad = cot_ref[ts, :].astype(F32)
        dh3, dg, db = norm_back(grad, xh, rstd, gain2)
        dz = dh3.astype(BF16)
        dz_s[ts, :] = dz
        dvec_ref[V_G + 2 : V_G + 3, :] += dg
        dvec_ref[V_B + 2 : V_B + 3, :] += db
        dvec_ref[V_FO : V_FO + 1, :] += jnp.sum(dz.astype(F32), axis=0, keepdims=True)
        dy2 = dh3
        for j, cs in enumerate(cols):
            du = (mm(dz, wout_ref[cs, :], 1, 1) * slope_s[:, cs]).astype(BF16)
            du_s[ts, cs] = du
            dvec_ref[V_FI + j : V_FI + j + 1, :] += jnp.sum(du.astype(F32), axis=0, keepdims=True)
            dy2 = dy2 + mm(du, win_ref[:, cs], 1, 1)
        xh2 = xh2_ref[ts, :].astype(F32)
        dh2, dg, db = norm_back(dy2, xh2, rs2_ref[ts, :], gain1)
        dh2_ref[ts, :] = dh2
        dvec_ref[V_G + 1 : V_G + 2, :] += dg
        dvec_ref[V_B + 1 : V_B + 2, :] += db

    mover.start("out", out_ref, out_h)
    mover.start("dh2", dh2_ref, dh2_h)
    for j, cs in enumerate(cols):
        rows = slice((G_OUT + j) * width, (G_OUT + j + 1) * width)
        put_halves(dw_ref, rows, mm(a_s[:, cs], dz_s[...], 0, 0))
        mover.start(rows.start, dw_ref.at[:, rows], dw_h.at[:, rows])
    for j, cs in enumerate(cols):
        rows = slice((G_IN + j) * width, (G_IN + j + 1) * width)
        put_halves(dw_ref, rows, mm(y2b_s[...], du_s[:, cs], 0, 0))
        mover.start(rows.start, dw_ref.at[:, rows], dw_h.at[:, rows])
    mover.finish()


def row_attend_back(
    k_ref, kt_ref, v_ref, q_ref, qt_ref, dc_ref, dct_ref, ctx_ref, lse_ref, mask_ref,
    delta, dqt, dq_ref, dk_ref, dv_ref, size, keys, query_start, after,
):
    @pl.loop(0, HEADS // 2)
    def _(pair):
        lanes = pl.ds(pl.multiple_of(pair * 2 * HEAD, 2 * HEAD), 2 * HEAD)
        both = dct_ref[lanes, :].astype(F32) * ctx_ref[lanes, :].astype(F32)
        for half in range(2):
            delta[half] = jnp.sum(both[half * HEAD : (half + 1) * HEAD], axis=0, keepdims=True)
        dqt[...] = jnp.zeros_like(dqt)
        for kb in range(keys // TB):
            ks, qs = slice(kb * TB, (kb + 1) * TB), slice(query_start(kb), size)
            dks, dvs = [], []
            for half in range(2):
                head = pair * 2 + half
                rows = pl.ds(pl.multiple_of(head * HEAD, HEAD), HEAD)
                s = mm(k_ref[ks, lanes], half_of(qt_ref[lanes, qs], half))
                p = jnp.exp2(s + mask_ref[ks, qs] - lse_ref[head, :, qs])
                dp = mm(v_ref[ks, lanes], half_of(dct_ref[lanes, qs], half))
                ds = (p * (dp - delta[half, :, qs])).astype(BF16)
                dvs.append(mm(p.astype(BF16), dc_ref[qs, lanes]))
                dks.append(mm(ds, q_ref[qs, lanes]))
                dqt[half * HEAD : (half + 1) * HEAD, qs] += mm(kt_ref[rows, ks], ds)
            first = lax.broadcasted_iota(jnp.int32, (TB, 2 * HEAD), 1) < HEAD
            dv_ref[ks, lanes] = jnp.where(first, dvs[0], dvs[1]).astype(BF16)
            dk_ref[ks, lanes] = (jnp.where(first, dks[0], dks[1]) * (1.0 / LOG2E)).astype(BF16)
        dq_ref[:, lanes] = (dqt[...] * SCALE).astype(BF16).T
        for place, act in enumerate(after):
            pl.when(pair == place)(act)


class Stream:
    def __init__(self, grads, sums, source, base, rows, slots, sems):
        dp, self.seq = lax.axis_index("dp"), lax.axis_size("seq")
        self.z = lax.axis_index("seq")
        self.core, x, y = lax.rem(dp, 2), lax.rem(dp // 2, 2), dp // 4
        self.near = {"dp": dp + 1 - 2 * self.core}
        by_x, by_y = {"dp": dp + 2 - 4 * x}, {"dp": dp + 4 - 8 * y}
        self.grads, self.sums, self.source, self.base, self.rows = grads, sums, source, base, rows
        self.slots, self.sems = slots, sems
        half, quarter, eighth = rows // 2, rows // 4, rows // 8
        self.unit = rows // (8 * self.seq)
        self.plan = []
        for part, (one, two, b1, b2) in enumerate(((x, y, by_x, by_y), (y, x, by_y, by_x))):
            start = part * half
            keep1, give1 = start + one * quarter, start + (1 - one) * quarter
            keep2, give2 = keep1 + two * eighth, keep1 + (1 - two) * eighth
            self.plan.append((b1, keep1, give1, b2, keep2, give2))

    def at(self, start, length):
        return pl.ds(pl.multiple_of(self.base + start, 16), length)

    def view(self, start, length):
        return self.grads.at[self.core, self.at(start, length)]

    def summed(self, start, length):
        return self.sums.at[self.core, self.at(start, length)]

    def own_copies(self):
        moves = [keep2 + self.z * self.unit for _, _, _, _, keep2, _ in self.plan]
        return [
            pltpu.make_async_copy(self.view(at, self.unit), self.summed(at, self.unit), self.sems[0].at[OWN + i])
            for i, at in enumerate(moves)
        ]

    def copies(self, step):
        rows, (s0, s1, s2, s3), seq = self.rows, self.slots, self.seq
        first = sum(COPIES[:step])
        sends, recvs = self.sems
        moves = []
        if step == 0:
            src = self.source.at[1 - self.core, self.at(0, rows)]
            moves.append((src, s0, self.near))
        if step == 7:
            moves.append((self.summed(0, rows), self.summed(0, rows), self.near))
        for part, (b1, keep1, give1, b2, keep2, give2) in enumerate(self.plan):
            if step == 1:
                moves.append((self.view(give1, rows // 4), s1.at[part], b1))
            if step == 2:
                moves.append((self.view(give2, rows // 8), s2.at[part], b2))
            if step == 5:
                moves.append((self.summed(keep2, rows // 8), self.summed(keep2, rows // 8), b2))
            if step == 6:
                moves.append((self.summed(keep1, rows // 4), self.summed(keep1, rows // 4), b1))
            for d in range(1, seq):
                to = lax.rem(self.z + d, seq)
                if step == 3:
                    moves.append((self.view(keep2 + to * self.unit, self.unit), s3.at[part, d - 1], {"seq": to}))
                if step == 4:
                    own = keep2 + self.z * self.unit
                    moves.append((self.view(own, self.unit), self.summed(own, self.unit), {"seq": to}))
        return [remote(*move[:2], sends, recvs, first + i, move[2]) for i, move in enumerate(moves)]

    def add(self, start, slots, length):
        unit = self.unit

        @pl.loop(0, length // unit)
        def _(i):
            place = pl.ds(pl.multiple_of(self.base + start + i * unit, 16), unit)
            total = self.grads[self.core, place, :].astype(F32)
            for slot in slots:
                total = total + slot[pl.ds(pl.multiple_of(i * unit, 16), unit), :].astype(F32)
            self.grads[self.core, place, :] = total.astype(BF16)

    def tick(self, step):
        if step:
            for copy in self.copies(step - 1):
                copy.wait()
        if step == 5:
            for copy in self.own_copies():
                copy.wait()
        s0, s1, s2, s3 = self.slots
        if step == 1:
            self.add(0, [s0], self.rows)
        for part, (_, keep1, _, _, keep2, _) in enumerate(self.plan):
            if step == 2:
                self.add(keep1, [s1.at[part]], self.rows // 4)
            if step == 3:
                self.add(keep2, [s2.at[part]], self.rows // 8)
            if step == 4:
                self.add(keep2 + self.z * self.unit, [s3.at[part, d] for d in range(self.seq - 1)], self.unit)
        if step < STEPS:
            for copy in self.copies(step):
                copy.start()
        if step == 4:
            for copy in self.own_copies():
                copy.start()


class VectorSum:
    def __init__(self, held, sems):
        dp, self.seq, self.z = lax.axis_index("dp"), lax.axis_size("seq"), lax.axis_index("seq")
        core, x, y = lax.rem(dp, 2), lax.rem(dp // 2, 2), dp // 4
        self.partners = [{"dp": dp + 1 - 2 * core}, {"dp": dp + 2 - 4 * x}, {"dp": dp + 4 - 8 * y}]
        self.held, self.sems = held, sems

    def copies(self, step):
        sends, recvs = self.sems
        if step < 3:
            return [remote(self.held.at[2 * step], self.held.at[2 * step + 1], sends, recvs, step, self.partners[step])]
        own = self.held.at[6 + self.z]
        return [remote(own, own, sends, recvs, 2 + d, {"seq": lax.rem(self.z + d, self.seq)}) for d in range(1, self.seq)]

    def tick(self, step):
        if step:
            for copy in self.copies(step - 1):
                copy.wait()
            if step < 4:
                to = 2 * step if step < 3 else 6 + self.z
                self.held[to] = self.held[2 * step - 2] + self.held[2 * step - 1]
        if step < 4:
            for copy in self.copies(step):
                copy.start()

    def total(self):
        values = self.held[6]
        for i in range(1, self.seq):
            values = values + self.held[6 + i]
        return values


BACK_INS = ("dh2", "co", "c2", "k2", "q2t", "v2", "q2", "k2t", "lse2", "mem", "ckv", "cq", "xh1", "rs1", "so",
            "ctx", "k", "qt", "v", "q", "kt", "lse", "x", "qkv")


def backward_kernel(tl_ref, sl_ref, gains, shifts, dvec_in, out_row_h, dwf_h, *rest):
    n = len(BACK_INS)
    hbm, rest = dict(zip(BACK_INS, rest[:n])), rest[n:]
    (out_h, dtok_h, dmem_h, grads_h, dvec_ref), rest = rest[:5], rest[5:]
    vmem, rest = dict(zip(BACK_INS, rest[:n])), rest[n:]
    (mask, mask2, delta, dqt, dc, dct, dq, dk, dv, dk2, dv2, dh1, y1b, dtok, dmem, grads, held), rest = rest[:17], rest[17:]
    slots, rest = [rest[4 * i : 4 * i + 4] for i in range(len(STREAMS))], rest[4 * len(STREAMS) :]
    sems, sends, recvs, xsends, xrecvs = rest
    x_ref, mem_ref, dh2_ref = vmem["x"], vmem["mem"], vmem["dh2"]
    c2_ref, ctx_ref = vmem["c2"], vmem["ctx"]
    size, width = x_ref.shape
    src = mem_ref.shape[0]
    seq = lax.axis_size("seq")
    row, dp = lax.axis_index("seq"), lax.axis_index("dp")
    blocks = [slice(t, t + TB) for t in range(0, size, TB)]
    mover = Mover(sems)
    for name in BACK_INS[:3]:
        mover.start(name, hbm[name], vmem[name])
    split = [(base * width, rows * width) for base, rows in STREAMS]
    streams = [
        Stream(grads, grads_h, dwf_h if i < 2 else grads, base, rows, slots[i], (sends.at[i], recvs.at[i]))
        for i, (base, rows) in enumerate(split)
    ]
    w_out, w_in, w_cross, w_qkv = (s.tick for s in streams)
    vectors = VectorSum(held, (sends.at[len(STREAMS)], recvs.at[len(STREAMS)]))
    core, x, y = streams[0].core, lax.rem(dp // 2, 2), dp // 4
    meet(
        [{"dp": dp + 1 - 2 * core}, {"dp": dp + 2 - 4 * x}, {"dp": dp + 4 - 8 * y}]
        + [{"seq": lax.rem(row + d, seq)} for d in range(1, seq)]
    )

    def exchange(source, target, kind):
        length = source.shape[0] // seq
        copies = []
        for d in range(1, seq):
            to = lax.rem(row + d, seq)
            rows = pl.ds(pl.multiple_of(to * length, 16), length)
            copies.append(remote(source.at[rows], target.at[row], xsends, xrecvs, kind * seq + d, {"seq": to}))
        for copy in copies:
            copy.start()
        mover.start((kind, "own"), source.at[pl.ds(pl.multiple_of(row * length, 16), length)], target.at[row])
        return copies

    w_out(0)
    w_in(0)
    mover.start("grads", dwf_h.at[core], grads.at[core, 0 : dwf_h.shape[1]])
    for name in BACK_INS[3:]:
        mover.start(name, hbm[name], vmem[name])
    gain0, shift0 = gains[0:1, :].astype(F32), shifts[0:1, :].astype(F32)

    def total(values):
        return jnp.sum(values.astype(F32), axis=0, keepdims=True)

    def gather(i, values):
        put_halves(grads, slice(i * width, (i + 1) * width), values)

    dvec_ref[...] = dvec_in[...]
    cross_mask(mask2, tl_ref[...], sl_ref[...], row, size, src)
    mover.wait("dh2", "co", "c2")
    for ts in blocks:
        da2 = dh2_ref[ts, :].astype(BF16)
        dc[ts, :] = mm(da2, vmem["co"][...], 1, 1).astype(BF16)
        dct[:, ts] = mm(vmem["co"][...], da2, 1, 1).astype(BF16)
        dvec_ref[V_CO : V_CO + 1, :] += total(da2)
    mover.wait("grads")
    w_out(1)
    gather(G_CO, mm(c2_ref[...], dh2_ref[...].astype(BF16)))
    w_in(1)
    mover.wait(*BACK_INS[3:9])
    row_attend_back(
        vmem["k2"], vmem["k2t"], vmem["v2"], vmem["q2"], vmem["q2t"], dc, dct, c2_ref, vmem["lse2"], mask2,
        delta, dqt, dq, dk2, dv2, size, src, lambda kb: 0,
        cross_ticks(w_out, w_in, w_cross, w_qkv),
    )
    out_copies = exchange(out_row_h, out_h, 0)
    dvec_ref[V_CV : V_CV + 1, :] = total(dv2[...])
    dvec_ref[V_CQ : V_CQ + 1, :] = total(dq[...])
    mover.wait("mem", "ckv", "cq", "xh1", "rs1", "so")
    gather(G_CK, mm(mem_ref[...], dk2[...], 0, 0))
    gather(G_CK + 1, mm(mem_ref[...], dv2[...], 0, 0))
    w_ckv = vmem["ckv"]
    dmem[...] = (
        mm(dk2[...], w_ckv[:, :width], 1, 1) + mm(dv2[...], w_ckv[:, width:], 1, 1)
    ).astype(BF16)
    for ts in blocks:
        dqb = dq[ts, :]
        dy1 = dh2_ref[ts, :] + mm(dqb, vmem["cq"][...], 1, 1)
        xh1 = vmem["xh1"][ts, :].astype(F32)
        y1b[ts, :] = (xh1 * gain0 + shift0).astype(BF16)
        dh, dg, db = norm_back(dy1, xh1, vmem["rs1"][ts, :], gain0)
        dvec_ref[V_G : V_G + 1, :] += dg
        dvec_ref[V_B : V_B + 1, :] += db
        dh1[ts, :] = dh
        dvec_ref[V_SO : V_SO + 1, :] += total(dh.astype(BF16))
    w_out(3)
    gather(G_CQ, mm(y1b[...], dq[...], 0, 0))
    self_mask(mask, tl_ref[...], row, size)
    for ts in blocks:
        da1 = dh1[ts, :].astype(BF16)
        dc[ts, :] = mm(da1, vmem["so"][...], 1, 1).astype(BF16)
        dct[:, ts] = mm(vmem["so"][...], da1, 1, 1).astype(BF16)
    w_in(3)
    mover.wait("ctx")
    gather(G_SO, mm(ctx_ref[...], dh1[...].astype(BF16)))
    w_cross(0)
    w_out(4)
    mover.wait("k", "qt", "v", "q", "kt", "lse")
    row_attend_back(
        vmem["k"], vmem["kt"], vmem["v"], vmem["q"], vmem["qt"], dc, dct, ctx_ref, vmem["lse"], mask,
        delta, dqt, dq, dk, dv, size, size, lambda kb: kb * TB,
        self_ticks(w_out, w_in, w_cross, w_qkv),
    )
    dvec_ref[V_Q : V_Q + 1, :] = total(dq[...])
    dvec_ref[V_V : V_V + 1, :] = total(dv[...])
    held[0] = dvec_ref[...]
    mover.wait("x", "qkv")
    for i, part in enumerate((dq, dk, dv)):
        gather(G_QKV + i, mm(x_ref[...], part[...], 0, 0))
    w_qkv(0)
    vectors.tick(0)
    wqkv_ref = vmem["qkv"]
    for ts in blocks:
        dtok[ts, :] = (
            dh1[ts, :]
            + mm(dq[ts, :], wqkv_ref[:, :width], 1, 1)
            + mm(dk[ts, :], wqkv_ref[:, width : 2 * width], 1, 1)
            + mm(dv[ts, :], wqkv_ref[:, 2 * width :], 1, 1)
        ).astype(BF16)
    w_qkv(1)
    vectors.tick(1)
    tok_copies = exchange(dtok, dtok_h, 1)
    mem_copies = exchange(dmem, dmem_h, 2)

    last_ticks(w_out, w_in, w_cross, w_qkv, vectors.tick)
    dvec_ref[...] = vectors.total()
    for copy in out_copies + tok_copies + mem_copies:
        copy.wait()
    mover.finish()


def cross_ticks(w_out, w_in, w_cross, w_qkv):
    def late():
        w_out(2)

    def last():
        w_in(2)

    return [lambda: None, lambda: None, late, last]


def self_ticks(w_out, w_in, w_cross, w_qkv):
    def first():
        w_in(4)
        w_cross(1)

    def second():
        w_out(5)

    def third():
        w_in(5)
        w_cross(2)
        w_out(6)

    def fourth():
        w_in(6)
        w_cross(3)
        w_out(7)

    return [first, second, third, fourth]


def last_ticks(w_out, w_in, w_cross, w_qkv, vectors):
    w_in(7)
    w_cross(4)
    w_out(8)
    w_qkv(2)
    vectors(2)
    w_cross(5)
    w_in(8)
    w_qkv(3)
    vectors(3)
    w_cross(6)
    w_qkv(4)
    vectors(4)
    w_cross(7)
    w_qkv(5)
    w_cross(8)
    w_qkv(6)
    w_qkv(7)
    w_qkv(8)


def unpack_kernel(grads_h, dvec_ref, dtok_h, dmem_h, *rest):
    outs, rest = rest[:18], rest[18:]
    mats, vecs = outs[:9], outs[9:]
    grads, dtok, dmem, rest = rest[0], rest[1], rest[2], rest[3:]
    wide, sems = rest[:9], rest[9]
    mover = Mover(sems)
    width = 2 * grads.shape[2]
    half = width // 2
    plan = ((0, G_QKV, 1, 3), (1, G_SO, 1, 1), (2, G_CQ, 1, 1), (3, G_CK, 1, 2), (4, G_CO, 1, 1), (5, G_IN, 1, 4), (6, G_OUT, 4, 1))
    for i, base, units, blocks in plan:
        rows = slice(base * width, (base + units * blocks) * width)
        mover.start(i, grads_h.at[:, rows], grads.at[:, rows])
    mover.start("tok", dtok_h, dtok)
    mover.start("mem", dmem_h, dmem)
    for i, base, units, blocks in plan:
        mover.wait(i)
        for b in range(blocks):
            for u in range(units):
                rows = slice((base + b + u) * width, (base + b + u + 1) * width)
                for c in range(2):
                    wide[i][u * width : (u + 1) * width, b * width + c * half : b * width + (c + 1) * half] = grads[c, rows, :].astype(F32)
        mover.start((i, "out"), wide[i], mats[i])
    for i, name, source in ((7, "tok", dtok), (8, "mem", dmem)):
        mover.wait(name)
        wide[i][...] = source[...].astype(F32)
        mover.start((i, "out"), wide[i], mats[i])
    place = 0
    for ref in vecs:
        if len(ref.shape) == 2:
            ref[...] = dvec_ref[place : place + ref.shape[0], :]
            place += ref.shape[0]
        else:
            for j in range(ref.shape[0] // width):
                ref[j * width : (j + 1) * width] = dvec_ref[place, :]
                place += 1
    mover.finish()


WHOLE = pl.BlockSpec(memory_space=pltpu.VMEM)


def call(kernel, ins, outs, scratch, name):
    return pl.pallas_call(
        kernel,
        out_shape=[jax.ShapeDtypeStruct(*o) for o in outs],
        in_specs=[WHOLE] * len(ins),
        out_specs=[WHOLE] * len(outs),
        scratch_shapes=[pltpu.VMEM(*s) for s in scratch],
        compiler_params=pltpu.CompilerParams(vmem_limit_bytes=60 * 2**20),
        name=name,
    )(*ins)


ANY = pl.BlockSpec(memory_space=pl.ANY)


def forward(tokens, memory, cot, tl, sl, small, wqkv, wso, wcq, wckv, wco):
    seq, block, d = tokens.shape
    t, s = seq * block, seq * memory.shape[1]
    tok, feat, row = ((t, d), BF16), ((d, t), BF16), ((HEADS, 1, t), F32)
    col, mem = ((t, 1), F32), ((s, d), BF16)
    kept = [tok, mem, tok, feat, tok, feat, tok, feat, row, tok, col,
            tok, feat, mem, ((d, s), BF16), mem, feat, row, ((t, d), F32), tok, col]
    weights = (wqkv, wso, wcq, wckv, wco)
    scratch = kept + [(w.shape, w.dtype) for w in weights]
    scratch += [((t, t), F32), ((s, t), F32), ((HEADS * AUG, t), BF16), ((HEADS * AUG, s), BF16), ((t, d), F32)]
    return pl.pallas_call(
        forward_kernel,
        out_shape=[jax.ShapeDtypeStruct(*o) for o in [tok] + kept],
        in_specs=[ANY] * 3 + [WHOLE] * (2 + len(small)) + [ANY] * 5,
        out_specs=[ANY] * FWD_OUTS,
        scratch_shapes=[pltpu.VMEM(*x) for x in scratch]
        + [pltpu.SemaphoreType.DMA((40,)), pltpu.SemaphoreType.DMA((3 * seq,)), pltpu.SemaphoreType.DMA((3 * seq,))],
        compiler_params=pltpu.CompilerParams(vmem_limit_bytes=60 * 2**20, collective_id=0, has_side_effects=True),
        name="forward",
    )(tokens, memory, cot, tl, sl, *small, *weights)


def ffn(y2, xh2, rs2, cot, small, win, wout):
    (t, d), f = y2.shape, win.shape[1]
    tok, wide = ((t, d), BF16), ((t, d), F32)
    dw = ((2, 2 * f, d // 2), BF16)
    return pl.pallas_call(
        ffn_kernel,
        out_shape=[jax.ShapeDtypeStruct(*o) for o in (tok, wide, dw, ((VECS, d), F32))],
        in_specs=[ANY] * 4 + [WHOLE] * len(small) + [ANY] * 2,
        out_specs=[ANY] * 3 + [WHOLE],
        scratch_shapes=[
            pltpu.VMEM(*x)
            for x in (wide, tok, ((t, 1), F32), tok, (win.shape, BF16), (wout.shape, BF16), tok, wide, dw,
                      ((t, f), BF16), ((t, f), BF16), ((TB, f), F32), tok, tok)
        ] + [pltpu.SemaphoreType.DMA((24,))],
        compiler_params=pltpu.CompilerParams(vmem_limit_bytes=60 * 2**20),
        name="ffn",
    )(y2, xh2, rs2, cot, *small, win, wout)


def backward(tl, sl, gains, shifts, dvec, out_row, dwf, ins):
    t, d = ins["x"].shape
    s = ins["mem"].shape[0]
    seq = lax.axis_size("seq")
    tok, mem = ((t, d), BF16), ((s, d), BF16)
    total = sum(rows for _, rows in STREAMS) * d
    grads = ((2, total, d // 2), BF16)
    scratch = [(ins[name].shape, ins[name].dtype) for name in BACK_INS]
    scratch += [((t, t), F32), ((s, t), F32), ((2, 1, t), F32), ((2 * HEAD, t), F32), tok, ((d, t), BF16),
                tok, tok, tok, mem, mem, ((t, d), F32), tok, tok, mem, grads, ((6 + seq, VECS, d), F32)]
    for _, rows in STREAMS:
        r, c = rows * d, d // 2
        scratch += [((r, c), BF16), ((2, r // 4, c), BF16), ((2, r // 8, c), BF16), ((2, seq - 1, r // (8 * seq), c), BF16)]
    steps = pltpu.SemaphoreType.DMA((len(STREAMS) + 1, OWN + 2))
    return pl.pallas_call(
        backward_kernel,
        out_shape=[
            jax.ShapeDtypeStruct((seq, t // seq, d), BF16),
            jax.ShapeDtypeStruct((seq, t // seq, d), BF16),
            jax.ShapeDtypeStruct((seq, s // seq, d), BF16),
            jax.ShapeDtypeStruct(*grads),
            jax.ShapeDtypeStruct((VECS, d), F32),
        ],
        in_specs=[WHOLE] * 5 + [ANY] * (2 + len(BACK_INS)),
        out_specs=[ANY] * 4 + [WHOLE],
        scratch_shapes=[pltpu.VMEM(*x) for x in scratch]
        + [pltpu.SemaphoreType.DMA((40,)), steps, steps, pltpu.SemaphoreType.DMA((3 * seq,)), pltpu.SemaphoreType.DMA((3 * seq,))],
        compiler_params=pltpu.CompilerParams(vmem_limit_bytes=62 * 2**20, collective_id=1, has_side_effects=True),
        name="backward",
    )(tl, sl, gains, shifts, dvec, out_row, dwf, *[ins[name] for name in BACK_INS])


def unpack(grads, dvec, dtok, dmem, d, f):
    mats = [(d, 3 * d), (d, d), (d, d), (d, 2 * d), (d, d), (d, f), (f, d), dtok.shape, dmem.shape]
    vecs = [(2 * d,), (d,), (d,), (d,), (d,), (f,), (d,), (3, d), (3, d)]
    outs = pl.pallas_call(
        unpack_kernel,
        out_shape=[jax.ShapeDtypeStruct(o, F32) for o in mats + vecs],
        in_specs=[ANY, WHOLE, ANY, ANY],
        out_specs=[ANY] * 9 + [WHOLE] * 9,
        scratch_shapes=[pltpu.VMEM(x.shape, x.dtype) for x in (grads, dtok, dmem)]
        + [pltpu.VMEM(m, F32) for m in mats] + [pltpu.SemaphoreType.DMA((24,))],
        compiler_params=pltpu.CompilerParams(vmem_limit_bytes=60 * 2**20),
        name="unpack",
    )(grads, dvec, dtok, dmem)
    d_qkv, d_so, d_cq, d_ckv, d_co, d_fi, d_fo, d_tok, d_mem = outs[:9]
    v_qv, v_so, v_cq, v_cv, v_co, v_fi, v_fo, d_gains, d_shifts = outs[9:]
    return (d_tok, d_mem, d_qkv, v_qv, d_so, v_so, d_cq, v_cq, d_ckv, v_cv, d_co, v_co, d_fi, v_fi, d_fo, v_fo, d_gains, d_shifts)


def layer_norm(values, gain, shift):
    center = values - jnp.mean(values, axis=-1, keepdims=True)
    spread = jnp.mean(center * center, axis=-1, keepdims=True)
    return center * lax.rsqrt(spread + 1e-05) * gain + shift


def doc_ids(lengths, size):
    ends = jnp.cumsum(lengths, axis=1)
    places = jnp.arange(size, dtype=jnp.int32)
    return jnp.sum((ends[:, None, :] <= places[None, :, None]).astype(jnp.int32), axis=2)


def block_width(key_total):
    return 512 if key_total % 512 == 0 else key_total


def contract_rows(left, right):
    return lax.dot_general(
        left, right, (((0,), (0,)), ((), ())), preferred_element_type=jnp.float32
    )


def contract_cols(left, right):
    return lax.dot_general(
        left, right, (((1,), (1,)), ((), ())), preferred_element_type=jnp.float32
    )


def block_scores(queries, keys, allowed, start_at, width_of, score_scale):
    key_block = lax.dynamic_slice_in_dim(keys, start_at, width_of, 1)
    scores = (
        jnp.einsum("rqhd,rkhd->rhqk", queries, key_block, preferred_element_type=jnp.float32)
        * score_scale
    )
    return jnp.where(allowed(start_at, width_of)[:, None], scores, -1000000000.0)


def attend_forward(queries, keys, values, allowed, skip_after, score_scale):
    row_count, query_count, head_count, head_size = queries.shape
    key_total = keys.shape[1]
    width_of = block_width(key_total)
    block_count = key_total // width_of

    def statistics(carried, block_index):
        start_at = block_index * width_of

        def statistics_work(state):
            running_max, running_sum = state
            scores = block_scores(queries, keys, allowed, start_at, width_of, score_scale)
            new_max = jnp.maximum(running_max, jnp.max(scores, axis=3))
            new_sum = running_sum * jnp.exp(running_max - new_max) + jnp.sum(
                jnp.exp(scores - new_max[..., None]), axis=3
            )
            return (new_max, new_sum)

        return (
            lax.cond(start_at > skip_after, lambda state: state, statistics_work, carried),
            None,
        )

    stat_shape = (row_count, head_count, query_count)
    start_state = (
        jnp.full(stat_shape, -1000000000.0, jnp.float32),
        jnp.zeros(stat_shape, jnp.float32),
    )
    block_numbers = jnp.arange(block_count, dtype=jnp.int32)
    (running_max, running_sum), _ = lax.scan(statistics, start_state, block_numbers)
    log_total = running_max + jnp.log(running_sum)

    def mixing(carried, block_index):
        start_at = block_index * width_of

        def mixing_work(accum):
            scores = block_scores(queries, keys, allowed, start_at, width_of, score_scale)
            probs = jnp.exp(scores - log_total[..., None]).astype(jnp.bfloat16)
            value_block = lax.dynamic_slice_in_dim(values, start_at, width_of, 1)
            return accum + jnp.einsum(
                "rhqk,rkhd->rqhd", probs, value_block, preferred_element_type=jnp.float32
            )

        return (lax.cond(start_at > skip_after, lambda accum: accum, mixing_work, carried), None)

    start_accum = jnp.zeros((row_count, query_count, head_count, head_size), jnp.float32)
    accum, _ = lax.scan(mixing, start_accum, block_numbers)
    return (accum, log_total)


def attend_back(
    queries, keys, values, allowed, skip_after, score_scale, log_total, grad_out, delta
):
    row_count, query_count, head_count, head_size = queries.shape
    key_total = keys.shape[1]
    width_of = block_width(key_total)
    block_count = key_total // width_of

    def step(block_index, state):
        start_at = block_index * width_of

        def step_work(inner):
            scores = block_scores(queries, keys, allowed, start_at, width_of, score_scale)
            probs = jnp.exp(scores - log_total[..., None])
            key_block = lax.dynamic_slice_in_dim(keys, start_at, width_of, 1)
            value_block = lax.dynamic_slice_in_dim(values, start_at, width_of, 1)
            grad_probs = jnp.einsum(
                "rqhd,rkhd->rhqk", grad_out, value_block, preferred_element_type=jnp.float32
            )
            grad_scores = (probs * (grad_probs - delta[..., None])).astype(jnp.bfloat16)
            grad_query = (
                inner[0]
                + jnp.einsum(
                    "rhqk,rkhd->rqhd", grad_scores, key_block, preferred_element_type=jnp.float32
                )
                * score_scale
            )
            key_part = (
                jnp.einsum(
                    "rhqk,rqhd->rkhd", grad_scores, queries, preferred_element_type=jnp.float32
                )
                * score_scale
            )
            value_part = jnp.einsum(
                "rhqk,rqhd->rkhd",
                probs.astype(jnp.bfloat16),
                grad_out,
                preferred_element_type=jnp.float32,
            )
            grad_keys = lax.dynamic_update_slice_in_dim(inner[1], key_part, start_at, 1)
            grad_values = lax.dynamic_update_slice_in_dim(inner[2], value_part, start_at, 1)
            return (grad_query, grad_keys, grad_values)

        return lax.cond(start_at > skip_after, lambda inner: inner, step_work, state)

    start_state = (jnp.zeros((row_count, query_count, head_count, head_size), jnp.float32),)
    start_state = start_state + (
        jnp.zeros((row_count, key_total, head_count, head_size), jnp.float32),
        jnp.zeros((row_count, key_total, head_count, head_size), jnp.float32),
    )
    return lax.fori_loop(0, block_count, step, start_state)


def blocks_on_device(
    tokens,
    memory,
    doc_lengths,
    src_lengths,
    cotangent,
    w_qkv,
    qv_bias,
    self_out,
    self_out_bias,
    cross_query,
    cross_q_bias,
    cross_kv,
    cross_v_bias,
    cross_out,
    cross_out_bias,
    ffn_in,
    ffn_in_bias,
    ffn_out,
    ffn_out_bias,
    norm_gains,
    norm_biases,
):
    row_count, block_len, model_width = tokens.shape
    src_block = memory.shape[1]
    seq_count = lax.axis_size("seq")
    row_length = block_len * seq_count
    src_length = src_block * seq_count
    score_scale = HEAD ** (-0.5)
    first_place = lax.axis_index("seq") * block_len
    last_place = first_place + block_len - 1
    target_ids = doc_ids(doc_lengths, row_length)
    source_ids = doc_ids(src_lengths, src_length)
    own_ids = lax.dynamic_slice_in_dim(target_ids, first_place, block_len, 1)
    own_places = first_place + jnp.arange(block_len, dtype=jnp.int32)

    def self_allowed(start_at, width_of):
        key_ids = lax.dynamic_slice_in_dim(target_ids, start_at, width_of, 1)
        key_places = start_at + jnp.arange(width_of, dtype=jnp.int32)
        return (own_ids[:, :, None] == key_ids[:, None, :]) & (
            key_places[None, None, :] <= own_places[None, :, None]
        )

    def cross_allowed(start_at, width_of):
        return (own_ids[:, :, None] == source_ids[:, None, :]) | (own_ids[:, :, None] == NDOC)

    def split_heads(array_in):
        return array_in.reshape(array_in.shape[0], array_in.shape[1], HEADS, HEAD)

    token_rows = row_count * block_len
    flat_tokens = tokens.reshape(token_rows, model_width)
    flat_memory = memory.reshape(row_count * src_block, model_width)
    pair_bias = qv_bias.astype(jnp.float32)
    gains = norm_gains.astype(jnp.float32)
    shifts = norm_biases.astype(jnp.float32)
    packed = jnp.dot(flat_tokens, w_qkv, preferred_element_type=jnp.float32)
    self_queries = (packed[:, :model_width] + pair_bias[:model_width]).astype(jnp.bfloat16)
    self_keys = (
        packed[:, model_width : 2 * model_width]
        .astype(jnp.bfloat16)
        .reshape(row_count, block_len, model_width)
    )
    self_values = (
        (packed[:, 2 * model_width :] + pair_bias[model_width:])
        .astype(jnp.bfloat16)
        .reshape(row_count, block_len, model_width)
    )
    memory_pair = jnp.dot(flat_memory, cross_kv, preferred_element_type=jnp.float32)
    cross_keys = (
        memory_pair[:, :model_width].astype(jnp.bfloat16).reshape(row_count, src_block, model_width)
    )
    cross_values = (
        (memory_pair[:, model_width:] + cross_v_bias.astype(jnp.float32))
        .astype(jnp.bfloat16)
        .reshape(row_count, src_block, model_width)
    )
    all_keys, all_values, all_ckeys, all_cvalues = (
        lax.all_gather(self_keys, "seq", axis=1, tiled=True),
        lax.all_gather(self_values, "seq", axis=1, tiled=True),
        lax.all_gather(cross_keys, "seq", axis=1, tiled=True),
        lax.all_gather(cross_values, "seq", axis=1, tiled=True),
    )
    query_heads = split_heads(self_queries.reshape(row_count, block_len, model_width))
    self_accum, self_log = attend_forward(
        query_heads,
        split_heads(all_keys),
        split_heads(all_values),
        self_allowed,
        last_place,
        score_scale,
    )
    context_low = self_accum.reshape(token_rows, model_width).astype(jnp.bfloat16)
    inputs_f = flat_tokens.astype(jnp.float32)
    first_sum = (
        inputs_f
        + jnp.dot(context_low, self_out, preferred_element_type=jnp.float32)
        + self_out_bias.astype(jnp.float32)
    )
    first_norm, first_pull = jax.vjp(layer_norm, first_sum, gains[0], shifts[0])
    first_low = first_norm.astype(jnp.bfloat16)
    cross_q_rows = (
        jnp.dot(first_low, cross_query, preferred_element_type=jnp.float32)
        + cross_q_bias.astype(jnp.float32)
    ).astype(jnp.bfloat16)
    cross_heads = split_heads(cross_q_rows.reshape(row_count, block_len, model_width))
    cross_accum, cross_log = attend_forward(
        cross_heads,
        split_heads(all_ckeys),
        split_heads(all_cvalues),
        cross_allowed,
        src_length,
        score_scale,
    )
    cross_low = cross_accum.reshape(token_rows, model_width).astype(jnp.bfloat16)
    second_sum = (
        first_norm
        + jnp.dot(cross_low, cross_out, preferred_element_type=jnp.float32)
        + cross_out_bias.astype(jnp.float32)
    )
    second_norm, second_pull = jax.vjp(layer_norm, second_sum, gains[1], shifts[1])
    second_low = second_norm.astype(jnp.bfloat16)
    hidden_pre = jnp.dot(
        second_low, ffn_in, preferred_element_type=jnp.float32
    ) + ffn_in_bias.astype(jnp.float32)
    hidden_low = jax.nn.silu(hidden_pre).astype(jnp.bfloat16)
    third_sum = (
        second_norm
        + jnp.dot(hidden_low, ffn_out, preferred_element_type=jnp.float32)
        + ffn_out_bias.astype(jnp.float32)
    )
    result, third_pull = jax.vjp(layer_norm, third_sum, gains[2], shifts[2])
    output = result.astype(jnp.bfloat16).reshape(row_count, block_len, model_width)
    grad_third, gain_three, shift_three = third_pull(
        cotangent.reshape(token_rows, model_width).astype(jnp.float32)
    )
    grad_branch = grad_third.astype(jnp.bfloat16)
    d_ffn_out = contract_rows(hidden_low, grad_branch)
    d_ffn_out_bias = jnp.sum(grad_branch.astype(jnp.float32), axis=0)
    grad_hidden = contract_cols(grad_branch, ffn_out)
    sigmoid_pre = jax.nn.sigmoid(hidden_pre)
    grad_pre = (grad_hidden * sigmoid_pre * (1.0 + hidden_pre * (1.0 - sigmoid_pre))).astype(
        jnp.bfloat16
    )
    d_ffn_in = contract_rows(second_low, grad_pre)
    d_ffn_in_bias = jnp.sum(grad_pre.astype(jnp.float32), axis=0)
    grad_second_norm = grad_third + contract_cols(grad_pre, ffn_in)
    back_keys, back_values, back_ckeys, back_cvalues = (
        all_keys,
        all_values,
        all_ckeys,
        all_cvalues,
    )
    grad_second, gain_two, shift_two = second_pull(grad_second_norm)
    grad_cross_branch = grad_second.astype(jnp.bfloat16)
    d_cross_out = contract_rows(cross_low, grad_cross_branch)
    d_cross_out_bias = jnp.sum(grad_cross_branch.astype(jnp.float32), axis=0)
    grad_cross_ctx = contract_cols(grad_cross_branch, cross_out).astype(jnp.bfloat16)
    grad_cross_heads = split_heads(grad_cross_ctx.reshape(row_count, block_len, model_width))
    cross_delta = jnp.swapaxes(
        jnp.sum(grad_cross_heads.astype(jnp.float32) * cross_accum, axis=3), 1, 2
    )
    grad_cq, grad_ck_all, grad_cv_all = attend_back(
        cross_heads,
        split_heads(back_ckeys),
        split_heads(back_cvalues),
        cross_allowed,
        src_length,
        score_scale,
        cross_log,
        grad_cross_heads,
        cross_delta,
    )
    grad_ck_own, grad_cv_own = (
        lax.psum_scatter(
            grad_ck_all.reshape(row_count, src_length, model_width).astype(jnp.bfloat16),
            "seq",
            scatter_dimension=1,
            tiled=True,
        ).astype(jnp.float32),
        lax.psum_scatter(
            grad_cv_all.reshape(row_count, src_length, model_width).astype(jnp.bfloat16),
            "seq",
            scatter_dimension=1,
            tiled=True,
        ).astype(jnp.float32),
    )
    grad_pair = jnp.concatenate(
        [
            grad_ck_own.reshape(row_count * src_block, model_width).astype(jnp.bfloat16),
            grad_cv_own.reshape(row_count * src_block, model_width).astype(jnp.bfloat16),
        ],
        axis=1,
    )
    d_cross_kv = contract_rows(flat_memory, grad_pair)
    d_cross_v_bias = jnp.sum(grad_pair[:, model_width:].astype(jnp.float32), axis=0)
    d_memory = contract_cols(grad_pair, cross_kv).reshape(row_count, src_block, model_width)
    grad_cq_low = grad_cq.reshape(token_rows, model_width).astype(jnp.bfloat16)
    d_cross_query = contract_rows(first_low, grad_cq_low)
    d_cross_q_bias = jnp.sum(grad_cq_low.astype(jnp.float32), axis=0)
    grad_first_norm = grad_second + contract_cols(grad_cq_low, cross_query)
    grad_first, gain_one, shift_one = first_pull(grad_first_norm)
    grad_self_branch = grad_first.astype(jnp.bfloat16)
    d_self_out = contract_rows(context_low, grad_self_branch)
    d_self_out_bias = jnp.sum(grad_self_branch.astype(jnp.float32), axis=0)
    grad_context = contract_cols(grad_self_branch, self_out).astype(jnp.bfloat16)
    grad_context_heads = split_heads(grad_context.reshape(row_count, block_len, model_width))
    self_delta = jnp.swapaxes(
        jnp.sum(grad_context_heads.astype(jnp.float32) * self_accum, axis=3), 1, 2
    )
    grad_q, grad_k_all, grad_v_all = attend_back(
        query_heads,
        split_heads(back_keys),
        split_heads(back_values),
        self_allowed,
        last_place,
        score_scale,
        self_log,
        grad_context_heads,
        self_delta,
    )
    grad_k_own, grad_v_own = (
        lax.psum_scatter(
            grad_k_all.reshape(row_count, row_length, model_width).astype(jnp.bfloat16),
            "seq",
            scatter_dimension=1,
            tiled=True,
        ).astype(jnp.float32),
        lax.psum_scatter(
            grad_v_all.reshape(row_count, row_length, model_width).astype(jnp.bfloat16),
            "seq",
            scatter_dimension=1,
            tiled=True,
        ).astype(jnp.float32),
    )
    grad_k_flat = grad_k_own.reshape(token_rows, model_width)
    grad_v_flat = grad_v_own.reshape(token_rows, model_width)
    grad_q_low = grad_q.reshape(token_rows, model_width).astype(jnp.bfloat16)
    grad_v_low = grad_v_flat.astype(jnp.bfloat16)
    grad_proj = jnp.concatenate([grad_q_low, grad_k_flat.astype(jnp.bfloat16), grad_v_low], axis=1)
    d_w_qkv = contract_rows(flat_tokens, grad_proj)
    d_qv_bias = jnp.concatenate(
        [
            jnp.sum(grad_q_low.astype(jnp.float32), axis=0),
            jnp.sum(grad_v_low.astype(jnp.float32), axis=0),
        ]
    )
    d_tokens = (grad_first + contract_cols(grad_proj, w_qkv)).reshape(
        row_count, block_len, model_width
    )
    d_norm_gains = jnp.stack([gain_one, gain_two, gain_three])
    d_norm_biases = jnp.stack([shift_one, shift_two, shift_three])
    (
        d_w_qkv,
        d_qv_bias,
        d_self_out,
        d_self_out_bias,
        d_cross_query,
        d_cross_q_bias,
        d_cross_kv,
        d_cross_v_bias,
        d_cross_out,
        d_cross_out_bias,
        d_ffn_in,
        d_ffn_in_bias,
        d_ffn_out,
        d_ffn_out_bias,
        d_norm_gains,
        d_norm_biases,
    ) = lax.psum(
        (
            d_w_qkv,
            d_qv_bias,
            d_self_out,
            d_self_out_bias,
            d_cross_query,
            d_cross_q_bias,
            d_cross_kv,
            d_cross_v_bias,
            d_cross_out,
            d_cross_out_bias,
            d_ffn_in,
            d_ffn_in_bias,
            d_ffn_out,
            d_ffn_out_bias,
            d_norm_gains,
            d_norm_biases,
        ),
        ("dp", "seq"),
    )
    return (
        output,
        d_tokens,
        d_memory,
        d_w_qkv,
        d_qv_bias,
        d_self_out,
        d_self_out_bias,
        d_cross_query,
        d_cross_q_bias,
        d_cross_kv,
        d_cross_v_bias,
        d_cross_out,
        d_cross_out_bias,
        d_ffn_in,
        d_ffn_in_bias,
        d_ffn_out,
        d_ffn_out_bias,
        d_norm_gains,
        d_norm_biases,
    )


def rows_on_device(
    tokens, memory, tl, sl, cotangent, w_qkv, qv_bias, self_out, self_out_bias, cross_query, cross_q_bias,
    cross_kv, cross_v_bias, cross_out, cross_out_bias, ffn_in, ffn_in_bias, ffn_out, ffn_out_bias, gains, shifts,
):
    small = (qv_bias, self_out_bias, cross_q_bias, cross_v_bias, cross_out_bias, gains, shifts)
    cot, *saved = forward(tokens, memory, cotangent, tl, sl, small, w_qkv, self_out, cross_query, cross_kv, cross_out)
    names = ("x", "mem", "q", "qt", "k", "kt", "v", "ctx", "lse", "xh1", "rs1",
             "q2", "q2t", "k2", "k2t", "v2", "c2", "lse2", "y2", "xh2", "rs2")
    ins = dict(zip(names, saved))
    ins |= {"qkv": w_qkv, "so": self_out, "cq": cross_query, "ckv": cross_kv, "co": cross_out}
    out_row, ins["dh2"], dwf, dvec = ffn(
        ins["y2"], ins["xh2"], ins["rs2"], cot, (ffn_in_bias, ffn_out_bias, gains, shifts), ffn_in, ffn_out
    )
    out, dtok, dmem, grads, dvec = backward(tl, sl, gains, shifts, dvec, out_row, dwf, ins)
    return (out,) + unpack(grads, dvec, dtok, dmem, ffn_in.shape[0], ffn_in.shape[1])


def on_device(tokens, *rest):
    if tokens.shape[0] == lax.axis_size("seq") and lax.axis_size("dp") == 8:
        return rows_on_device(tokens, *rest)
    return blocks_on_device(tokens, *rest)


def solution(mesh):
    in_specs = (
        P("dp", "seq", None),
        P("dp", "seq", None),
        P("dp", None),
        P("dp", None),
        P("dp", "seq", None),
        P(),
        P(),
        P(),
        P(),
        P(),
        P(),
        P(),
        P(),
        P(),
        P(),
        P(),
        P(),
        P(),
        P(),
        P(),
        P(),
    )
    out_specs = (
        P("dp", "seq", None),
        P("dp", "seq", None),
        P("dp", "seq", None),
        P(),
        P(),
        P(),
        P(),
        P(),
        P(),
        P(),
        P(),
        P(),
        P(),
        P(),
        P(),
        P(),
        P(),
        P(),
        P(),
    )
    return jax.shard_map(
        on_device, mesh=mesh, in_specs=in_specs, out_specs=out_specs, check_vma=False
    )
```

profile of v0, /device:TPU:0, one launch (start us, length us, event | category | flops | bytes accessed | tf_op | source)
XLA Modules:
  0.0 258.5 jit_solution(1998414551906137673)
XLA Ops:
  0.7 64.5 %forward.1 = (bf16[1024,512]{1,0:T(8,128)(2,1)}, bf16[1024,512]{1,0:T(8,128)(2,1)}, bf16[256,512]{1,0:T(8,128)(2,1)}, bf16[1024,512]{1,0:T(8,128)(2,1)}, bf16[51...) custom-call(bf16[4,256,512]{2,1,0:T(8,128)(2,1)} %tok_ref.1, ...), custom_call_target="tpu_custom_call" | custom-call | tf_op jit(solution)/shard_map/forward/pallas_call | solution.py:779
  65.1 26.1 %ffn.1 = (bf16[1024,512]{1,0:T(8,128)(2,1)}, f32[1024,512]{1,0:T(8,128)}, bf16[2,4096,256]{2,1,0:T(8,128)(2,1)}, f32[24,512]{1,0:T(8,128)}) custom-call(f32[1024,512]{1,0:T(8,128)} %get-tuple-element.68.y2_h, bf16[1024,512]{1,0:T(8,128)(2,1)} %get-tuple-element.69.xh2_h, f32[1024,1]{1,0:T(8,128)} %get-tuple-element.70.rs2_h, ...), custom_call_target="tpu_custom_call" | custom-call | tf_op jit(solution)/shard_map/ffn/pallas_call | solution.py:795
  91.3 155.4 %backward.1 = (bf16[4,256,512]{2,1,0:T(8,128)(2,1)}, bf16[4,256,512]{2,1,0:T(8,128)(2,1)}, bf16[4,64,512]{2,1,0:T(8,128)(2,1)}, bf16[2,8192,256]{2,1,0:T(8,128)(2,1)}, f32[24,512]{1,0:T(8,128)}) custom-call(s32[4,32]{1,0:T(4,128)} %tl_ref.3, s32[4,32]{1,0:T(4,128)} %sl_ref.3, bf16[3,512]{1,0:T(4,128)(2,1)} %gains.5, bf16[3,512]{1,0:T(4,128)(2,1)} %shifts.5, ...), custom_call_target="tpu_custom_call" | custom-call | tf_op jit(solution)/shard_map/backward/pallas_call | solution.py:824
  246.7 0.0 copy-start
  246.7 10.8 %unpack.1 = (f32[512,1536]{1,0:T(8,128)}, f32[512,512]{1,0:T(8,128)}, f32[512,512]{1,0:T(8,128)}, f32[512,1024]{1,0:T(8,128)}, f32[512,512]{1,0:T(8,128)}, /*ind...) custom-call(bf16[2,8192,256]{2,1,0:T(8,128)(2,1)} %get-tuple-element, ...), custom_call_target="tpu_custom_call" | custom-call | tf_op jit(solution)/shard_map/unpack/pallas_call | solution.py:845
  257.5 0.0 copy-done
  257.5 1.0 copy.41
Async XLA Ops:
  246.7 10.8 %copy-start = (bf16[4,256,512]{2,1,0:T(8,128)(2,1)S(1)}, bf16[4,256,512]{2,1,0:T(8,128)(2,1)}, u32[]{:S(2)}) copy-start(bf16[4,256,512]{2,1,0:T(8,128)(2,1)} %get-tuple-element.136) | copy-start | bytes 3145732
where the time goes:
time: 259 us
  Pallas kernels  257 us (99%)
    pallas_call x1, Pallas kernels, backward(): pl.pallas_call(backward_kernel, out_shape=[jax.ShapeDtypeStruct((seq, t /...  155 us
    pallas_call x1, Pallas kernels, forward(): pl.pallas_call(forward_kernel, out_shape=[jax.ShapeDtypeStruct(*o) for o...  64.5 us
    pallas_call x1, Pallas kernels, ffn(): pl.pallas_call(ffn_kernel, out_shape=[jax.ShapeDtypeStruct(*o) for o in (...  26.1 us
    pallas_call x1, Pallas kernels, unpack(): pl.pallas_call(unpack_kernel, out_shape=[jax.ShapeDtypeStruct(o, F32) for...  10.8 us

commit v1 on v0

--- a/solution.py
+++ b/solution.py
@@ -19,8 +19,10 @@
 
 V_Q, V_V, V_SO, V_CQ, V_CV, V_CO, V_FI, V_FO, V_G, V_B = 0, 1, 2, 3, 4, 5, 6, 10, 11, 14
 VECS = 24
-G_IN, G_OUT, G_CO, G_CQ, G_CK, G_SO, G_QKV = 0, 4, 8, 9, 10, 12, 13
-STREAMS = ((G_OUT, 4), (G_IN, 4), (G_CO, 5), (G_QKV, 3))
+G_IN, G_OUT, G_CO, G_CK, G_CQ, G_SO, G_QKV = 0, 4, 8, 9, 11, 12, 13
+STREAMS = ((G_OUT, 20, 4), (G_IN, 16, 4), (G_CO, 20, 3), (G_CQ, 23, 2), (G_QKV, 16, 2), (G_QKV + 2, 18, 1))
+UNITS, ALL_UNITS = 16, 25
+PIECES = 8
 STEPS = 8
 COPIES = (1, 2, 2, 6, 6, 2, 2, 1)
 OWN = sum(COPIES)
@@ -278,87 +280,12 @@
     mover.finish()
 
 
-def put_halves(ref, rows, values):
-    half = values.shape[1] // 2
-    ref[0, rows, :] = values[:, :half].astype(BF16)
-    ref[1, rows, :] = values[:, half:].astype(BF16)
-
-
-def ffn_kernel(
-    y2_h, xh2_h, rs2_h, cot_h, bfi, bfo, gains, shifts, win_h, wout_h,
-    out_h, dh2_h, dw_h, dvec_ref,
-    y2_ref, xh2_ref, rs2_ref, cot_ref, win_ref, wout_ref, out_ref, dh2_ref, dw_ref,
-    a_s, du_s, slope_s, y2b_s, dz_s, sems,
-):
-    size, width = y2_ref.shape
-    inner = win_ref.shape[1]
-    cols = [slice(j, j + width) for j in range(0, inner, width)]
-    mover = Mover(sems)
-    for name, src, dst in (
-        ("y2", y2_h, y2_ref), ("win", win_h, win_ref), ("wout", wout_h, wout_ref),
-        ("cot", cot_h, cot_ref), ("xh2", xh2_h, xh2_ref), ("rs2", rs2_h, rs2_ref),
-    ):
-        mover.start(name, src, dst)
-    gain2, shift2, gain1 = gains[2:3, :].astype(F32), shifts[2:3, :].astype(F32), gains[1:2, :].astype(F32)
-    dvec_ref[...] = jnp.zeros_like(dvec_ref)
-    mover.wait("y2", "win", "wout", "cot", "xh2", "rs2")
-
-    @pl.loop(0, size // TB)
-    def _(tb):
-        ts = pl.ds(pl.multiple_of(tb * TB, TB), TB)
-        y2 = y2_ref[ts, :]
-        y2b = y2.astype(BF16)
-        y2b_s[ts, :] = y2b
-        h3 = y2 + vec_of(bfo, 0, width)
-        for j, cs in enumerate(cols):
-            u = mm(y2b, win_ref[:, cs]) + vec_of(bfi, j * width, width)
-            sg = 0.5 * jnp.tanh(0.5 * u) + 0.5
-            act = u * sg
-            slope_s[:, cs] = sg + act * (1.0 - sg)
-            act = act.astype(BF16)
-            a_s[ts, cs] = act
-            h3 = h3 + mm(act, wout_ref[cs, :])
-        xh, rstd = normalize(h3)
-        out_ref[ts, :] = (xh * gain2 + shift2).astype(BF16)
-        grad = cot_ref[ts, :].astype(F32)
-        dh3, dg, db = norm_back(grad, xh, rstd, gain2)
-        dz = dh3.astype(BF16)
-        dz_s[ts, :] = dz
-        dvec_ref[V_G + 2 : V_G + 3, :] += dg
-        dvec_ref[V_B + 2 : V_B + 3, :] += db
-        dvec_ref[V_FO : V_FO + 1, :] += jnp.sum(dz.astype(F32), axis=0, keepdims=True)
-        dy2 = dh3
-        for j, cs in enumerate(cols):
-            du = (mm(dz, wout_ref[cs, :], 1, 1) * slope_s[:, cs]).astype(BF16)
-            du_s[ts, cs] = du
-            dvec_ref[V_FI + j : V_FI + j + 1, :] += jnp.sum(du.astype(F32), axis=0, keepdims=True)
-            dy2 = dy2 + mm(du, win_ref[:, cs], 1, 1)
-        xh2 = xh2_ref[ts, :].astype(F32)
-        dh2, dg, db = norm_back(dy2, xh2, rs2_ref[ts, :], gain1)
-        dh2_ref[ts, :] = dh2
-        dvec_ref[V_G + 1 : V_G + 2, :] += dg
-        dvec_ref[V_B + 1 : V_B + 2, :] += db
-
-    mover.start("out", out_ref, out_h)
-    mover.start("dh2", dh2_ref, dh2_h)
-    for j, cs in enumerate(cols):
-        rows = slice((G_OUT + j) * width, (G_OUT + j + 1) * width)
-        put_halves(dw_ref, rows, mm(a_s[:, cs], dz_s[...], 0, 0))
-        mover.start(rows.start, dw_ref.at[:, rows], dw_h.at[:, rows])
-    for j, cs in enumerate(cols):
-        rows = slice((G_IN + j) * width, (G_IN + j + 1) * width)
-        put_halves(dw_ref, rows, mm(y2b_s[...], du_s[:, cs], 0, 0))
-        mover.start(rows.start, dw_ref.at[:, rows], dw_h.at[:, rows])
-    mover.finish()
-
-
 def row_attend_back(
     k_ref, kt_ref, v_ref, q_ref, qt_ref, dc_ref, dct_ref, ctx_ref, lse_ref, mask_ref,
     delta, dqt, dq_ref, dk_ref, dv_ref, size, keys, query_start, after,
 ):
-    @pl.loop(0, HEADS // 2)
-    def _(pair):
-        lanes = pl.ds(pl.multiple_of(pair * 2 * HEAD, 2 * HEAD), 2 * HEAD)
+    for pair in range(HEADS // 2):
+        lanes = slice(pair * 2 * HEAD, (pair + 1) * 2 * HEAD)
         both = dct_ref[lanes, :].astype(F32) * ctx_ref[lanes, :].astype(F32)
         for half in range(2):
             delta[half] = jnp.sum(both[half * HEAD : (half + 1) * HEAD], axis=0, keepdims=True)
@@ -368,7 +295,7 @@
             dks, dvs = [], []
             for half in range(2):
                 head = pair * 2 + half
-                rows = pl.ds(pl.multiple_of(head * HEAD, HEAD), HEAD)
+                rows = slice(head * HEAD, (head + 1) * HEAD)
                 s = mm(k_ref[ks, lanes], half_of(qt_ref[lanes, qs], half))
                 p = jnp.exp2(s + mask_ref[ks, qs] - lse_ref[head, :, qs])
                 dp = mm(v_ref[ks, lanes], half_of(dct_ref[lanes, qs], half))
@@ -379,19 +306,18 @@
             first = lax.broadcasted_iota(jnp.int32, (TB, 2 * HEAD), 1) < HEAD
             dv_ref[ks, lanes] = jnp.where(first, dvs[0], dvs[1]).astype(BF16)
             dk_ref[ks, lanes] = (jnp.where(first, dks[0], dks[1]) * (1.0 / LOG2E)).astype(BF16)
+            after(pair, kb)
         dq_ref[:, lanes] = (dqt[...] * SCALE).astype(BF16).T
-        for place, act in enumerate(after):
-            pl.when(pair == place)(act)
 
 
 class Stream:
-    def __init__(self, grads, sums, source, base, rows, slots, sems):
+    def __init__(self, grads, sums, base, give, rows, slots, sems):
         dp, self.seq = lax.axis_index("dp"), lax.axis_size("seq")
         self.z = lax.axis_index("seq")
         self.core, x, y = lax.rem(dp, 2), lax.rem(dp // 2, 2), dp // 4
         self.near = {"dp": dp + 1 - 2 * self.core}
         by_x, by_y = {"dp": dp + 2 - 4 * x}, {"dp": dp + 4 - 8 * y}
-        self.grads, self.sums, self.source, self.base, self.rows = grads, sums, source, base, rows
+        self.grads, self.sums, self.base, self.give, self.rows = grads, sums, base, give, rows
         self.slots, self.sems = slots, sems
         half, quarter, eighth = rows // 2, rows // 4, rows // 8
         self.unit = rows // (8 * self.seq)
@@ -406,7 +332,7 @@
         return pl.ds(pl.multiple_of(self.base + start, 16), length)
 
     def view(self, start, length):
-        return self.grads.at[self.core, self.at(start, length)]
+        return self.grads.at[self.at(start, length)]
 
     def summed(self, start, length):
         return self.sums.at[self.core, self.at(start, length)]
@@ -424,8 +350,7 @@
         sends, recvs = self.sems
         moves = []
         if step == 0:
-            src = self.source.at[1 - self.core, self.at(0, rows)]
-            moves.append((src, s0, self.near))
+            moves.append((self.grads.at[self.give : self.give + rows], s0, self.near))
         if step == 7:
             moves.append((self.summed(0, rows), self.summed(0, rows), self.near))
         for part, (b1, keep1, give1, b2, keep2, give2) in enumerate(self.plan):
@@ -447,15 +372,19 @@
         return [remote(*move[:2], sends, recvs, first + i, move[2]) for i, move in enumerate(moves)]
 
     def add(self, start, slots, length):
-        unit = self.unit
-
-        @pl.loop(0, length // unit)
-        def _(i):
-            place = pl.ds(pl.multiple_of(self.base + start + i * unit, 16), unit)
-            total = self.grads[self.core, place, :].astype(F32)
+        chunk = min(length, self.rows // 8)
+
+        def at(i):
+            place = pl.ds(pl.multiple_of(self.base + start + i * chunk, 16), chunk)
+            total = self.grads[place, :].astype(F32)
             for slot in slots:
-                total = total + slot[pl.ds(pl.multiple_of(i * unit, 16), unit), :].astype(F32)
-            self.grads[self.core, place, :] = total.astype(BF16)
+                total = total + slot[pl.ds(pl.multiple_of(i * chunk, 16), chunk), :].astype(F32)
+            self.grads[place, :] = total.astype(BF16)
+
+        if length == chunk:
+            at(0)
+        else:
+            pl.loop(0, length // chunk)(at)
 
     def tick(self, step):
         if step:
@@ -477,7 +406,7 @@
         if step < STEPS:
             for copy in self.copies(step):
                 copy.start()
-        if step == 4:
+        if step == 4 and step < STEPS:
             for copy in self.own_copies():
                 copy.start()
 
@@ -514,36 +443,68 @@
         return values
 
 
-BACK_INS = ("dh2", "co", "c2", "k2", "q2t", "v2", "q2", "k2t", "lse2", "mem", "ckv", "cq", "xh1", "rs1", "so",
-            "ctx", "k", "qt", "v", "q", "kt", "lse", "x", "qkv")
-
-
-def backward_kernel(tl_ref, sl_ref, gains, shifts, dvec_in, out_row_h, dwf_h, *rest):
-    n = len(BACK_INS)
-    hbm, rest = dict(zip(BACK_INS, rest[:n])), rest[n:]
-    (out_h, dtok_h, dmem_h, grads_h, dvec_ref), rest = rest[:5], rest[5:]
-    vmem, rest = dict(zip(BACK_INS, rest[:n])), rest[n:]
-    (mask, mask2, delta, dqt, dc, dct, dq, dk, dv, dk2, dv2, dh1, y1b, dtok, dmem, grads, held), rest = rest[:17], rest[17:]
+INS = ("y2", "win", "cot", "wout", "xh2", "rs2", "co", "c2", "k2", "q2t", "v2", "k2t", "lse2", "mem", "ckv",
+       "rs1", "kt", "k", "v", "q", "x", "q2", "xh1", "cq", "so", "qkv", "qt", "ctx", "lse")
+HELD = INS[:17]
+POOL = 14
+
+
+def main_kernel(plan, tl_ref, sl_ref, bfi, bfo, gains, shifts, *rest):
+    n = len(INS)
+    hbm, rest = dict(zip(INS, rest[:n])), rest[n:]
+    (out_h, dtok_h, dmem_h, sums_h, dvec_ref), rest = rest[:5], rest[5:]
+    vmem, rest = dict(zip(HELD, rest[: len(HELD)])), rest[len(HELD) :]
+    pool, rest = rest[:POOL], rest[POOL:]
+    (out_row, dh1, mask, mask2, delta, dqt, dct, dk2, dv2, dmem, grads, held), rest = rest[:12], rest[12:]
     slots, rest = [rest[4 * i : 4 * i + 4] for i in range(len(STREAMS))], rest[4 * len(STREAMS) :]
     sems, sends, recvs, xsends, xrecvs = rest
-    x_ref, mem_ref, dh2_ref = vmem["x"], vmem["mem"], vmem["dh2"]
-    c2_ref, ctx_ref = vmem["c2"], vmem["ctx"]
-    size, width = x_ref.shape
-    src = mem_ref.shape[0]
-    seq = lax.axis_size("seq")
-    row, dp = lax.axis_index("seq"), lax.axis_index("dp")
+    size, width = vmem["y2"].shape
+    inner = vmem["win"].shape[1]
+    src = vmem["mem"].shape[0]
+    acts, dus, slopes, (y2b, dz_s) = pool[0:4], pool[4:8], pool[8:12], pool[12:14]
+    vmem |= dict(zip(("k", "v", "q", "x"), pool[0:4]))
+    dq, dk, dv, dc = pool[4:8]
+    vmem |= {"q2": pool[8], "xh1": pool[9], "qt": vmem["q2t"], "ctx": vmem["c2"], "lse": vmem["lse2"]}
+    wout = vmem["wout"]
+    vmem |= {"cq": wout.at[0:width], "so": wout.at[width : 2 * width], "qkv": vmem["win"].at[:, : 3 * width]}
+    y1b, dtok = y2b, dz_s
+    cols = [slice(j, j + width) for j in range(0, inner, width)]
     blocks = [slice(t, t + TB) for t in range(0, size, TB)]
+    seq, row, dp = lax.axis_size("seq"), lax.axis_index("seq"), lax.axis_index("dp")
     mover = Mover(sems)
-    for name in BACK_INS[:3]:
-        mover.start(name, hbm[name], vmem[name])
-    split = [(base * width, rows * width) for base, rows in STREAMS]
+
+    def load(*names):
+        for name in names:
+            mover.start(name, hbm[name], vmem[name])
+
+    load(*HELD)
+    split = [(keep * width, give * width, rows * width) for keep, give, rows in STREAMS]
     streams = [
-        Stream(grads, grads_h, dwf_h if i < 2 else grads, base, rows, slots[i], (sends.at[i], recvs.at[i]))
-        for i, (base, rows) in enumerate(split)
+        Stream(grads, sums_h, *where, slots[i], (sends.at[i], recvs.at[i])) for i, where in enumerate(split)
     ]
-    w_out, w_in, w_cross, w_qkv = (s.tick for s in streams)
     vectors = VectorSum(held, (sends.at[len(STREAMS)], recvs.at[len(STREAMS)]))
     core, x, y = streams[0].core, lax.rem(dp // 2, 2), dp // 4
+    pieces = []
+
+    def send_piece(step):
+        length = size // seq
+        part = length // PIECES
+        copies = []
+        for d in range(1, seq):
+            to = lax.rem(row + d, seq)
+            rows = pl.ds(pl.multiple_of(to * length + step * part, 16), part)
+            place = dtok_h.at[row, step * part : (step + 1) * part]
+            copies.append(remote(dtok.at[rows], place, xsends, xrecvs, (3 + step) * seq + d, {"seq": to}))
+        for copy in copies:
+            copy.start()
+        pieces.extend(copies)
+
+    ticks = [s.tick for s in streams] + [vectors.tick, send_piece]
+
+    def act(place):
+        for stream, step in plan.get(place, ()):
+            ticks[stream](step)
+
     meet(
         [{"dp": dp + 1 - 2 * core}, {"dp": dp + 2 - 4 * x}, {"dp": dp + 4 - 8 * y}]
         + [{"seq": lax.rem(row + d, seq)} for d in range(1, seq)]
@@ -561,153 +522,191 @@
         mover.start((kind, "own"), source.at[pl.ds(pl.multiple_of(row * length, 16), length)], target.at[row])
         return copies
 
-    w_out(0)
-    w_in(0)
-    mover.start("grads", dwf_h.at[core], grads.at[core, 0 : dwf_h.shape[1]])
-    for name in BACK_INS[3:]:
-        mover.start(name, hbm[name], vmem[name])
-    gain0, shift0 = gains[0:1, :].astype(F32), shifts[0:1, :].astype(F32)
+    gives = {keep + i: give + i for keep, give, rows in STREAMS for i in range(rows)}
+
+    def gather(i, values):
+        half = width // 2
+        keep, give = i * width, gives[i] * width
+        left = pl.multiple_of(jnp.where(core == 0, keep, give), width)
+        right = pl.multiple_of(jnp.where(core == 0, give, keep), width)
+        grads[pl.ds(left, width), :] = values[:, :half].astype(BF16)
+        grads[pl.ds(right, width), :] = values[:, half:].astype(BF16)
 
     def total(values):
         return jnp.sum(values.astype(F32), axis=0, keepdims=True)
 
-    def gather(i, values):
-        put_halves(grads, slice(i * width, (i + 1) * width), values)
-
-    dvec_ref[...] = dvec_in[...]
+    def count(i, values):
+        dvec_ref[i : i + 1, :] += values
+
+    gain0, shift0 = gains[0:1, :].astype(F32), shifts[0:1, :].astype(F32)
+    gain1, gain2, shift2 = gains[1:2, :].astype(F32), gains[2:3, :].astype(F32), shifts[2:3, :].astype(F32)
+    dvec_ref[...] = jnp.zeros_like(dvec_ref)
+    mover.wait("y2", "win", "cot", "wout")
+    y2_ref, win = vmem["y2"], vmem["win"]
+
+    @pl.loop(0, size // TB)
+    def _(tb):
+        ts = pl.ds(pl.multiple_of(tb * TB, TB), TB)
+        y2 = y2_ref[ts, :]
+        low = y2.astype(BF16)
+        y2b[ts, :] = low
+        h3 = y2 + vec_of(bfo, 0, width)
+        for j, cs in enumerate(cols):
+            u = mm(low, win[:, cs]) + vec_of(bfi, j * width, width)
+            sg = 0.5 * jnp.tanh(0.5 * u) + 0.5
+            a = u * sg
+            slopes[j][ts, :] = (sg + a * (1.0 - sg)).astype(BF16)
+            a = a.astype(BF16)
+            acts[j][ts, :] = a
+            h3 = h3 + mm(a, wout[cs, :])
+        xh, rstd = normalize(h3)
+        out_row[ts, :] = (xh * gain2 + shift2).astype(BF16)
+        dh3, dg, db = norm_back(vmem["cot"][ts, :].astype(F32), xh, rstd, gain2)
+        y2_ref[ts, :] = dh3
+        dz = dh3.astype(BF16)
+        dz_s[ts, :] = dz
+        count(V_G + 2, dg)
+        count(V_B + 2, db)
+        count(V_FO, total(dz))
+
+    out_copies = exchange(out_row, out_h, 0)
+    for j in range(len(cols)):
+        gather(G_OUT + j, mm(acts[j][...], dz_s[...], 0, 0))
+    act("ffn_out")
+    load("k", "v", "q", "x")
+    mover.wait("xh2", "rs2")
+    for tb, ts in enumerate(blocks):
+        dz = dz_s[ts, :]
+        dy2 = y2_ref[ts, :]
+        for j, cs in enumerate(cols):
+            du = (mm(dz, wout[cs, :], 1, 1) * slopes[j][ts, :].astype(F32)).astype(BF16)
+            dus[j][ts, :] = du
+            count(V_FI + j, total(du))
+            dy2 = dy2 + mm(du, win[:, cs], 1, 1)
+            if j == 1:
+                act(("ffn", tb, 0))
+        dh2, dg, db = norm_back(dy2, vmem["xh2"][ts, :].astype(F32), vmem["rs2"][ts, :], gain1)
+        y2_ref[ts, :] = dh2
+        count(V_G + 1, dg)
+        count(V_B + 1, db)
+        act(("ffn", tb, 1))
+
+    load("q2", "xh1", "cq", "so", "qkv")
+    dh2_ref = y2_ref
+    for j in range(len(cols)):
+        gather(G_IN + j, mm(y2b[...], dus[j][...], 0, 0))
+        act(("in", j))
+    act("ffn_in")
     cross_mask(mask2, tl_ref[...], sl_ref[...], row, size, src)
-    mover.wait("dh2", "co", "c2")
-    for ts in blocks:
+    act("mask2")
+    mover.wait("co", "c2")
+    for tb, ts in enumerate(blocks):
         da2 = dh2_ref[ts, :].astype(BF16)
         dc[ts, :] = mm(da2, vmem["co"][...], 1, 1).astype(BF16)
         dct[:, ts] = mm(vmem["co"][...], da2, 1, 1).astype(BF16)
-        dvec_ref[V_CO : V_CO + 1, :] += total(da2)
-    mover.wait("grads")
-    w_out(1)
-    gather(G_CO, mm(c2_ref[...], dh2_ref[...].astype(BF16)))
-    w_in(1)
-    mover.wait(*BACK_INS[3:9])
+        count(V_CO, total(da2))
+        act(("cin", tb))
+    act("cross_in")
+    gather(G_CO, mm(vmem["c2"][...], dh2_ref[...].astype(BF16)))
+    act("cross_out")
+    mover.wait("k2", "q2t", "v2", "k2t", "lse2", "q2")
     row_attend_back(
-        vmem["k2"], vmem["k2t"], vmem["v2"], vmem["q2"], vmem["q2t"], dc, dct, c2_ref, vmem["lse2"], mask2,
-        delta, dqt, dq, dk2, dv2, size, src, lambda kb: 0,
-        cross_ticks(w_out, w_in, w_cross, w_qkv),
-    )
-    out_copies = exchange(out_row_h, out_h, 0)
-    dvec_ref[V_CV : V_CV + 1, :] = total(dv2[...])
-    dvec_ref[V_CQ : V_CQ + 1, :] = total(dq[...])
+        vmem["k2"], vmem["k2t"], vmem["v2"], vmem["q2"], vmem["q2t"], dc, dct, vmem["c2"], vmem["lse2"], mask2,
+        delta, dqt, dq, dk2, dv2, size, src, lambda kb: 0, lambda i, j: act(("cross", i, j)),
+    )
+    load("qt", "ctx", "lse")
+    count(V_CV, total(dv2[...]))
+    count(V_CQ, total(dq[...]))
     mover.wait("mem", "ckv", "cq", "xh1", "rs1", "so")
-    gather(G_CK, mm(mem_ref[...], dk2[...], 0, 0))
-    gather(G_CK + 1, mm(mem_ref[...], dv2[...], 0, 0))
+    gather(G_CK, mm(vmem["mem"][...], dk2[...], 0, 0))
+    gather(G_CK + 1, mm(vmem["mem"][...], dv2[...], 0, 0))
+    act("ck")
     w_ckv = vmem["ckv"]
-    dmem[...] = (
-        mm(dk2[...], w_ckv[:, :width], 1, 1) + mm(dv2[...], w_ckv[:, width:], 1, 1)
-    ).astype(BF16)
-    for ts in blocks:
-        dqb = dq[ts, :]
-        dy1 = dh2_ref[ts, :] + mm(dqb, vmem["cq"][...], 1, 1)
+    dmem[...] = (mm(dk2[...], w_ckv[:, :width], 1, 1) + mm(dv2[...], w_ckv[:, width:], 1, 1)).astype(BF16)
+    act("memory")
+    mem_copies = exchange(dmem, dmem_h, 2)
+    for tb, ts in enumerate(blocks):
+        dy1 = dh2_ref[ts, :] + mm(dq[ts, :], vmem["cq"][...], 1, 1)
         xh1 = vmem["xh1"][ts, :].astype(F32)
         y1b[ts, :] = (xh1 * gain0 + shift0).astype(BF16)
         dh, dg, db = norm_back(dy1, xh1, vmem["rs1"][ts, :], gain0)
-        dvec_ref[V_G : V_G + 1, :] += dg
-        dvec_ref[V_B : V_B + 1, :] += db
+        count(V_G, dg)
+        count(V_B, db)
         dh1[ts, :] = dh
-        dvec_ref[V_SO : V_SO + 1, :] += total(dh.astype(BF16))
-    w_out(3)
+        count(V_SO, total(dh.astype(BF16)))
+        act(("nrm", tb))
+    act("norm")
     gather(G_CQ, mm(y1b[...], dq[...], 0, 0))
+    act("query")
     self_mask(mask, tl_ref[...], row, size)
-    for ts in blocks:
+    act("mask")
+    mover.wait("ctx")
+    gather(G_SO, mm(vmem["ctx"][...], dh1[...].astype(BF16)))
+    act("self_out")
+    for tb, ts in enumerate(blocks):
         da1 = dh1[ts, :].astype(BF16)
         dc[ts, :] = mm(da1, vmem["so"][...], 1, 1).astype(BF16)
         dct[:, ts] = mm(vmem["so"][...], da1, 1, 1).astype(BF16)
-    w_in(3)
-    mover.wait("ctx")
-    gather(G_SO, mm(ctx_ref[...], dh1[...].astype(BF16)))
-    w_cross(0)
-    w_out(4)
+        act(("sin", tb))
+    act("self_in")
     mover.wait("k", "qt", "v", "q", "kt", "lse")
     row_attend_back(
-        vmem["k"], vmem["kt"], vmem["v"], vmem["q"], vmem["qt"], dc, dct, ctx_ref, vmem["lse"], mask,
-        delta, dqt, dq, dk, dv, size, size, lambda kb: kb * TB,
-        self_ticks(w_out, w_in, w_cross, w_qkv),
-    )
-    dvec_ref[V_Q : V_Q + 1, :] = total(dq[...])
-    dvec_ref[V_V : V_V + 1, :] = total(dv[...])
-    held[0] = dvec_ref[...]
+        vmem["k"], vmem["kt"], vmem["v"], vmem["q"], vmem["qt"], dc, dct, vmem["ctx"], vmem["lse"], mask,
+        delta, dqt, dq, dk, dv, size, size, lambda kb: kb * TB, lambda i, j: act(("self", i, j)),
+    )
     mover.wait("x", "qkv")
     for i, part in enumerate((dq, dk, dv)):
-        gather(G_QKV + i, mm(x_ref[...], part[...], 0, 0))
-    w_qkv(0)
-    vectors.tick(0)
-    wqkv_ref = vmem["qkv"]
-    for ts in blocks:
+        gather(G_QKV + i, mm(vmem["x"][...], part[...], 0, 0))
+    act("qkv")
+    count(V_Q, total(dq[...]))
+    count(V_V, total(dv[...]))
+    held[0] = dvec_ref[...]
+    act("vectors")
+    w_qkv = vmem["qkv"]
+    for tb, ts in enumerate(blocks):
         dtok[ts, :] = (
             dh1[ts, :]
-            + mm(dq[ts, :], wqkv_ref[:, :width], 1, 1)
-            + mm(dk[ts, :], wqkv_ref[:, width : 2 * width], 1, 1)
-            + mm(dv[ts, :], wqkv_ref[:, 2 * width :], 1, 1)
+            + mm(dq[ts, :], w_qkv[:, :width], 1, 1)
+            + mm(dk[ts, :], w_qkv[:, width : 2 * width], 1, 1)
+            + mm(dv[ts, :], w_qkv[:, 2 * width :], 1, 1)
         ).astype(BF16)
-    w_qkv(1)
-    vectors.tick(1)
-    tok_copies = exchange(dtok, dtok_h, 1)
-    mem_copies = exchange(dmem, dmem_h, 2)
-
-    last_ticks(w_out, w_in, w_cross, w_qkv, vectors.tick)
+        act(("tok", tb))
+    own = pl.ds(pl.multiple_of(row * (size // seq), 16), size // seq)
+    mover.start("own tokens", dtok.at[own], dtok_h.at[row])
+    act("tokens")
+    act("end")
     dvec_ref[...] = vectors.total()
-    for copy in out_copies + tok_copies + mem_copies:
+    for copy in out_copies + pieces + mem_copies:
         copy.wait()
     mover.finish()
 
 
-def cross_ticks(w_out, w_in, w_cross, w_qkv):
-    def late():
-        w_out(2)
-
-    def last():
-        w_in(2)
-
-    return [lambda: None, lambda: None, late, last]
-
-
-def self_ticks(w_out, w_in, w_cross, w_qkv):
-    def first():
-        w_in(4)
-        w_cross(1)
-
-    def second():
-        w_out(5)
-
-    def third():
-        w_in(5)
-        w_cross(2)
-        w_out(6)
-
-    def fourth():
-        w_in(6)
-        w_cross(3)
-        w_out(7)
-
-    return [first, second, third, fourth]
-
-
-def last_ticks(w_out, w_in, w_cross, w_qkv, vectors):
-    w_in(7)
-    w_cross(4)
-    w_out(8)
-    w_qkv(2)
-    vectors(2)
-    w_cross(5)
-    w_in(8)
-    w_qkv(3)
-    vectors(3)
-    w_cross(6)
-    w_qkv(4)
-    vectors(4)
-    w_cross(7)
-    w_qkv(5)
-    w_cross(8)
-    w_qkv(6)
-    w_qkv(7)
-    w_qkv(8)
+PLAN = {
+    "ffn_out": [(0, 0)],
+    ("ffn", 1, 0): [(0, 1)],
+    "ffn_in": [(1, 0)],
+    "mask2": [(0, 2)],
+    "cross_in": [(1, 1)],
+    ("cross", 2, 0): [(0, 3)],
+    "ck": [(2, 0)],
+    ("nrm", 2): [(1, 2), (2, 1)],
+    "self_out": [(3, 0), (0, 4)],
+    "self_in": [(3, 1)],
+    ("self", 0, 0): [(1, 3)],
+    ("self", 1, 0): [(2, 2)],
+    ("self", 1, 2): [(0, 5)],
+    ("self", 1, 3): [(3, 2)],
+    ("self", 2, 2): [(2, 3)],
+    ("self", 3, 0): [(1, 4)],
+    ("self", 3, 1): [(0, 6)],
+    ("self", 3, 2): [(3, 3)],
+    "qkv": [(4, 0), (5, 0)],
+    ("tok", 1): [(2, 4)],
+    ("tok", 2): [(4, 1), (5, 1)],
+    "end": [(0, 7), (1, 5), (0, 8), (4, 2), (3, 4), (5, 2), (1, 6), (6, 2), (2, 5), (7, 0), (4, 3), (5, 3), (3, 5), (1, 7), (7, 1), (6, 3), (4, 4), (2, 6), (5, 4), (1, 8), (3, 6), (4, 5), (7, 2), (6, 4), (2, 7), (5, 5), (2, 8), (7, 3), (3, 7), (4, 6), (3, 8), (7, 4), (5, 6), (4, 7), (7, 5), (5, 7), (4, 8), (5, 8), (7, 6), (7, 7)],
+    "vectors": [(6, 0)],
+    "tokens": [(6, 1)],
+}
 
 
 def unpack_kernel(grads_h, dvec_ref, dtok_h, dmem_h, *rest):
@@ -788,55 +787,34 @@
     )(tokens, memory, cot, tl, sl, *small, *weights)
 
 
-def ffn(y2, xh2, rs2, cot, small, win, wout):
-    (t, d), f = y2.shape, win.shape[1]
-    tok, wide = ((t, d), BF16), ((t, d), F32)
-    dw = ((2, 2 * f, d // 2), BF16)
-    return pl.pallas_call(
-        ffn_kernel,
-        out_shape=[jax.ShapeDtypeStruct(*o) for o in (tok, wide, dw, ((VECS, d), F32))],
-        in_specs=[ANY] * 4 + [WHOLE] * len(small) + [ANY] * 2,
-        out_specs=[ANY] * 3 + [WHOLE],
-        scratch_shapes=[
-            pltpu.VMEM(*x)
-            for x in (wide, tok, ((t, 1), F32), tok, (win.shape, BF16), (wout.shape, BF16), tok, wide, dw,
-                      ((t, f), BF16), ((t, f), BF16), ((TB, f), F32), tok, tok)
-        ] + [pltpu.SemaphoreType.DMA((24,))],
-        compiler_params=pltpu.CompilerParams(vmem_limit_bytes=60 * 2**20),
-        name="ffn",
-    )(y2, xh2, rs2, cot, *small, win, wout)
-
-
-def backward(tl, sl, gains, shifts, dvec, out_row, dwf, ins):
-    t, d = ins["x"].shape
+def main(tl, sl, small, ins):
+    t, d = ins["y2"].shape
     s = ins["mem"].shape[0]
     seq = lax.axis_size("seq")
-    tok, mem = ((t, d), BF16), ((s, d), BF16)
-    total = sum(rows for _, rows in STREAMS) * d
-    grads = ((2, total, d // 2), BF16)
-    scratch = [(ins[name].shape, ins[name].dtype) for name in BACK_INS]
-    scratch += [((t, t), F32), ((s, t), F32), ((2, 1, t), F32), ((2 * HEAD, t), F32), tok, ((d, t), BF16),
-                tok, tok, tok, mem, mem, ((t, d), F32), tok, tok, mem, grads, ((6 + seq, VECS, d), F32)]
-    for _, rows in STREAMS:
+    tok, mem, wide = ((t, d), BF16), ((s, d), BF16), ((t, d), F32)
+    scratch = [(ins[name].shape, ins[name].dtype) for name in HELD] + [tok] * POOL
+    scratch += [tok, wide, ((t, t), F32), ((s, t), F32), ((2, 1, t), F32), ((2 * HEAD, t), F32), ((d, t), BF16),
+                mem, mem, mem, ((ALL_UNITS * d, d // 2), BF16), ((6 + seq, VECS, d), F32)]
+    for _, _, rows in STREAMS:
         r, c = rows * d, d // 2
         scratch += [((r, c), BF16), ((2, r // 4, c), BF16), ((2, r // 8, c), BF16), ((2, seq - 1, r // (8 * seq), c), BF16)]
     steps = pltpu.SemaphoreType.DMA((len(STREAMS) + 1, OWN + 2))
     return pl.pallas_call(
-        backward_kernel,
+        functools.partial(main_kernel, PLAN),
         out_shape=[
             jax.ShapeDtypeStruct((seq, t // seq, d), BF16),
             jax.ShapeDtypeStruct((seq, t // seq, d), BF16),
             jax.ShapeDtypeStruct((seq, s // seq, d), BF16),
-            jax.ShapeDtypeStruct(*grads),
+            jax.ShapeDtypeStruct((2, UNITS * d, d // 2), BF16),
             jax.ShapeDtypeStruct((VECS, d), F32),
         ],
-        in_specs=[WHOLE] * 5 + [ANY] * (2 + len(BACK_INS)),
+        in_specs=[WHOLE] * 6 + [ANY] * len(INS),
         out_specs=[ANY] * 4 + [WHOLE],
         scratch_shapes=[pltpu.VMEM(*x) for x in scratch]
-        + [pltpu.SemaphoreType.DMA((40,)), steps, steps, pltpu.SemaphoreType.DMA((3 * seq,)), pltpu.SemaphoreType.DMA((3 * seq,))],
+        + [pltpu.SemaphoreType.DMA((40,)), steps, steps] + [pltpu.SemaphoreType.DMA(((3 + PIECES) * seq,))] * 2,
         compiler_params=pltpu.CompilerParams(vmem_limit_bytes=62 * 2**20, collective_id=1, has_side_effects=True),
-        name="backward",
-    )(tl, sl, gains, shifts, dvec, out_row, dwf, *[ins[name] for name in BACK_INS])
+        name="main",
+    )(tl, sl, *small, *[ins[name] for name in INS])
 
 
 def unpack(grads, dvec, dtok, dmem, d, f):
@@ -1314,16 +1292,13 @@
     cross_kv, cross_v_bias, cross_out, cross_out_bias, ffn_in, ffn_in_bias, ffn_out, ffn_out_bias, gains, shifts,
 ):
     small = (qv_bias, self_out_bias, cross_q_bias, cross_v_bias, cross_out_bias, gains, shifts)
-    cot, *saved = forward(tokens, memory, cotangent, tl, sl, small, w_qkv, self_out, cross_query, cross_kv, cross_out)
-    names = ("x", "mem", "q", "qt", "k", "kt", "v", "ctx", "lse", "xh1", "rs1",
+    saved = forward(tokens, memory, cotangent, tl, sl, small, w_qkv, self_out, cross_query, cross_kv, cross_out)
+    names = ("cot", "x", "mem", "q", "qt", "k", "kt", "v", "ctx", "lse", "xh1", "rs1",
              "q2", "q2t", "k2", "k2t", "v2", "c2", "lse2", "y2", "xh2", "rs2")
     ins = dict(zip(names, saved))
-    ins |= {"qkv": w_qkv, "so": self_out, "cq": cross_query, "ckv": cross_kv, "co": cross_out}
-    out_row, ins["dh2"], dwf, dvec = ffn(
-        ins["y2"], ins["xh2"], ins["rs2"], cot, (ffn_in_bias, ffn_out_bias, gains, shifts), ffn_in, ffn_out
-    )
-    out, dtok, dmem, grads, dvec = backward(tl, sl, gains, shifts, dvec, out_row, dwf, ins)
-    return (out,) + unpack(grads, dvec, dtok, dmem, ffn_in.shape[0], ffn_in.shape[1])
+    ins |= {"qkv": w_qkv, "so": self_out, "cq": cross_query, "ckv": cross_kv, "co": cross_out, "win": ffn_in, "wout": ffn_out}
+    out, dtok, dmem, sums, dvec = main(tl, sl, (ffn_in_bias, ffn_out_bias, gains, shifts), ins)
+    return (out,) + unpack(sums, dvec, dtok, dmem, ffn_in.shape[0], ffn_in.shape[1])
 
 
 def on_device(tokens, *rest):

time: 259 us -> 209 us (0.81)
  Pallas kernels: 257 us -> 204 us
    pallas_call x2 -> x1, Pallas kernels: 182 us -> 129 us  [main(): pl.pallas_call(functools.partial(main_kernel, PLAN), out_shape=[jax.Shape...]
where the time goes in v1:
time: 209 us; the launch traced here: 206 us
  Pallas kernels  204 us (98%)
    pallas_call x1, Pallas kernels, main(): pl.pallas_call(functools.partial(main_kernel, PLAN), out_shape=[jax.Shape...  129 us
    pallas_call x1, Pallas kernels, forward(): pl.pallas_call(forward_kernel, out_shape=[jax.ShapeDtypeStruct(*o) for o...  64.8 us
    pallas_call x1, Pallas kernels, unpack(): pl.pallas_call(unpack_kernel, out_shape=[jax.ShapeDtypeStruct(o, F32) for...  10.8 us

profile of v1, /device:TPU:0, one launch (start us, length us, event | category | flops | bytes accessed | tf_op | source)
XLA Modules:
  0.0 206.2 jit_solution(6725755495670673891)
XLA Ops:
  0.7 64.8 %forward.1 = (bf16[1024,512]{1,0:T(8,128)(2,1)}, bf16[1024,512]{1,0:T(8,128)(2,1)}, bf16[256,512]{1,0:T(8,128)(2,1)}, bf16[1024,512]{1,0:T(8,128)(2,1)}, bf16[51...) custom-call(bf16[4,256,512]{2,1,0:T(8,128)(2,1)} %tok_ref.1, ...), custom_call_target="tpu_custom_call" | custom-call | tf_op jit(solution)/shard_map/forward/pallas_call | solution.py:778
  65.5 128.6 %main.1 = (bf16[4,256,512]{2,1,0:T(8,128)(2,1)}, bf16[4,256,512]{2,1,0:T(8,128)(2,1)}, bf16[4,64,512]{2,1,0:T(8,128)(2,1)}, bf16[2,8192,256]{2,1,0:T(8,128)(2,1)}, f32[24,512]{1,0:T(8,128)}) custom-call(s32[4,32]{1,0:T(4,128)} %tl_ref.3, s32[4,32]{1,0:T(4,128)} %sl_ref.3, bf16[2048]{0:T(1024)(128)(2,1)} %bfi.1, bf16[512]{0:T(512)(128)(2,1)} %bfo.1, ...), custom_call_target="tpu_custom_call" | custom-call | tf_op jit(solution)/shard_map/main/pallas_call | solution.py:802
  194.1 0.0 copy-start
  194.1 10.8 %unpack.1 = (f32[512,1536]{1,0:T(8,128)}, f32[512,512]{1,0:T(8,128)}, f32[512,512]{1,0:T(8,128)}, f32[512,1024]{1,0:T(8,128)}, f32[512,512]{1,0:T(8,128)}, /*ind...) custom-call(bf16[2,8192,256]{2,1,0:T(8,128)(2,1)} %get-tuple-element, ...), custom_call_target="tpu_custom_call" | custom-call | tf_op jit(solution)/shard_map/unpack/pallas_call | solution.py:823
  204.9 0.0 copy-done
  205.0 1.0 copy.41
Async XLA Ops:
  194.1 10.8 %copy-start = (bf16[4,256,512]{2,1,0:T(8,128)(2,1)S(1)}, bf16[4,256,512]{2,1,0:T(8,128)(2,1)}, u32[]{:S(2)}) copy-start(bf16[4,256,512]{2,1,0:T(8,128)(2,1)} %get-tuple-element.128) | copy-start | bytes 3145732

commit v2 on v1

--- a/solution.py
+++ b/solution.py
@@ -16,11 +16,12 @@
 F32 = jnp.float32
 BF16 = jnp.bfloat16
 TB = 256
+FB = 512
 
 V_Q, V_V, V_SO, V_CQ, V_CV, V_CO, V_FI, V_FO, V_G, V_B = 0, 1, 2, 3, 4, 5, 6, 10, 11, 14
 VECS = 24
 G_IN, G_OUT, G_CO, G_CK, G_CQ, G_SO, G_QKV = 0, 4, 8, 9, 11, 12, 13
-STREAMS = ((G_OUT, 20, 4), (G_IN, 16, 4), (G_CO, 20, 3), (G_CQ, 23, 2), (G_QKV, 16, 2), (G_QKV + 2, 18, 1))
+STREAMS = ((4, 20, 4), (0, 16, 4), (8, 20, 3), (11, 23, 2), (13, 16, 2), (15, 18, 1))
 UNITS, ALL_UNITS = 16, 25
 PIECES = 8
 STEPS = 8
@@ -107,9 +108,8 @@
 
 
 def row_attend(k_ref, qt_ref, vt_ref, mask_ref, ctx_ref, lse_ref, size, key_end):
-    @pl.loop(0, HEADS // 2)
-    def _(pair):
-        lanes = pl.ds(pl.multiple_of(pair * 2 * HEAD, 2 * HEAD), 2 * HEAD)
+    for pair in range(HEADS // 2):
+        lanes = slice(pair * 2 * HEAD, (pair + 1) * 2 * HEAD)
         for half in range(2):
             head = pair * 2 + half
             for qb in range(size // TB):
@@ -118,9 +118,9 @@
                 s = s + mask_ref[0:ke, qs]
                 m = jnp.max(s, axis=0, keepdims=True)
                 p = jnp.exp2(s - m).astype(BF16)
-                o = mm(vt_ref[pl.ds(pl.multiple_of(head * AUG, 16), AUG), 0:ke], p)
+                o = mm(vt_ref[head * AUG : (head + 1) * AUG, 0:ke], p)
                 total = o[HEAD : HEAD + 1]
-                ctx_ref[pl.ds(pl.multiple_of(head * HEAD, HEAD), HEAD), qs] = (
+                ctx_ref[head * HEAD : (head + 1) * HEAD, qs] = (
                     o[:HEAD] * (1.0 / total)
                 ).astype(BF16)
                 lse_ref[head, :, qs] = m + jnp.log2(total)
@@ -247,8 +247,8 @@
     for i in (7, 8):
         mover.start(i, kept[i], outs[1 + i])
     mover.wait("wso", "wcq")
-    for tb in range(blocks):
-        ts = slice(tb * TB, (tb + 1) * TB)
+    for tb in range(size // FB):
+        ts = slice(tb * FB, (tb + 1) * FB)
         h1 = x_ref[ts, :].astype(F32) + mm(ctx_ref[:, ts].T, wso_ref[...]) + vec_of(bso, 0, width)
         xh, rstd = normalize(h1)
         xh1_ref[ts, :] = xh.astype(BF16)
@@ -264,8 +264,8 @@
     for i in (16, 17):
         mover.start(i, kept[i], outs[1 + i])
     mover.wait("wco")
-    for tb in range(blocks):
-        ts = slice(tb * TB, (tb + 1) * TB)
+    for tb in range(size // FB):
+        ts = slice(tb * FB, (tb + 1) * FB)
         h2 = y1[ts, :] + mm(c2_ref[:, ts].T, wco_ref[...]) + vec_of(bco, 0, width)
         xh, rstd = normalize(h2)
         xh2_ref[ts, :] = xh.astype(BF16)
@@ -486,20 +486,23 @@
     core, x, y = streams[0].core, lax.rem(dp // 2, 2), dp // 4
     pieces = []
 
-    def send_piece(step):
-        length = size // seq
-        part = length // PIECES
-        copies = []
-        for d in range(1, seq):
-            to = lax.rem(row + d, seq)
-            rows = pl.ds(pl.multiple_of(to * length + step * part, 16), part)
-            place = dtok_h.at[row, step * part : (step + 1) * part]
-            copies.append(remote(dtok.at[rows], place, xsends, xrecvs, (3 + step) * seq + d, {"seq": to}))
-        for copy in copies:
-            copy.start()
-        pieces.extend(copies)
-
-    ticks = [s.tick for s in streams] + [vectors.tick, send_piece]
+    def piece_sender(source, target, kind):
+        def send_piece(step):
+            length = size // seq
+            part = length // PIECES
+            copies = []
+            for d in range(1, seq):
+                to = lax.rem(row + d, seq)
+                rows = pl.ds(pl.multiple_of(to * length + step * part, 16), part)
+                place = target.at[row, step * part : (step + 1) * part]
+                copies.append(remote(source.at[rows], place, xsends, xrecvs, (kind + step) * seq + d, {"seq": to}))
+            for copy in copies:
+                copy.start()
+            pieces.extend(copies)
+
+        return send_piece
+
+    ticks = [s.tick for s in streams] + [vectors.tick, piece_sender(dtok, dtok_h, 1), piece_sender(out_row, out_h, 1 + PIECES)]
 
     def act(place):
         for stream, step in plan.get(place, ()):
@@ -544,9 +547,8 @@
     mover.wait("y2", "win", "cot", "wout")
     y2_ref, win = vmem["y2"], vmem["win"]
 
-    @pl.loop(0, size // TB)
-    def _(tb):
-        ts = pl.ds(pl.multiple_of(tb * TB, TB), TB)
+    for tb in range(size // FB):
+        ts = slice(tb * FB, (tb + 1) * FB)
         y2 = y2_ref[ts, :]
         low = y2.astype(BF16)
         y2b[ts, :] = low
@@ -569,13 +571,15 @@
         count(V_B + 2, db)
         count(V_FO, total(dz))
 
-    out_copies = exchange(out_row, out_h, 0)
+    own = pl.ds(pl.multiple_of(row * (size // seq), 16), size // seq)
+    mover.start("own output", out_row.at[own], out_h.at[row])
     for j in range(len(cols)):
         gather(G_OUT + j, mm(acts[j][...], dz_s[...], 0, 0))
+        act(("out", j))
     act("ffn_out")
     load("k", "v", "q", "x")
     mover.wait("xh2", "rs2")
-    for tb, ts in enumerate(blocks):
+    for tb, ts in enumerate([slice(t, t + FB) for t in range(0, size, FB)]):
         dz = dz_s[ts, :]
         dy2 = y2_ref[ts, :]
         for j, cs in enumerate(cols):
@@ -583,13 +587,13 @@
             dus[j][ts, :] = du
             count(V_FI + j, total(du))
             dy2 = dy2 + mm(du, win[:, cs], 1, 1)
-            if j == 1:
-                act(("ffn", tb, 0))
+            if j < 3:
+                act(("ffn", tb, j))
         dh2, dg, db = norm_back(dy2, vmem["xh2"][ts, :].astype(F32), vmem["rs2"][ts, :], gain1)
         y2_ref[ts, :] = dh2
         count(V_G + 1, dg)
         count(V_B + 1, db)
-        act(("ffn", tb, 1))
+        act(("ffn", tb, 3))
 
     load("q2", "xh1", "cq", "so", "qkv")
     dh2_ref = y2_ref
@@ -624,7 +628,7 @@
     w_ckv = vmem["ckv"]
     dmem[...] = (mm(dk2[...], w_ckv[:, :width], 1, 1) + mm(dv2[...], w_ckv[:, width:], 1, 1)).astype(BF16)
     act("memory")
-    mem_copies = exchange(dmem, dmem_h, 2)
+    mem_copies = exchange(dmem, dmem_h, 0)
     for tb, ts in enumerate(blocks):
         dy1 = dh2_ref[ts, :] + mm(dq[ts, :], vmem["cq"][...], 1, 1)
         xh1 = vmem["xh1"][ts, :].astype(F32)
@@ -657,6 +661,7 @@
     mover.wait("x", "qkv")
     for i, part in enumerate((dq, dk, dv)):
         gather(G_QKV + i, mm(vmem["x"][...], part[...], 0, 0))
+        act(("qkv", i))
     act("qkv")
     count(V_Q, total(dq[...]))
     count(V_V, total(dv[...]))
@@ -671,41 +676,44 @@
             + mm(dv[ts, :], w_qkv[:, 2 * width :], 1, 1)
         ).astype(BF16)
         act(("tok", tb))
-    own = pl.ds(pl.multiple_of(row * (size // seq), 16), size // seq)
     mover.start("own tokens", dtok.at[own], dtok_h.at[row])
     act("tokens")
     act("end")
     dvec_ref[...] = vectors.total()
-    for copy in out_copies + pieces + mem_copies:
+    for copy in pieces + mem_copies:
         copy.wait()
     mover.finish()
 
 
 PLAN = {
-    "ffn_out": [(0, 0)],
-    ("ffn", 1, 0): [(0, 1)],
-    "ffn_in": [(1, 0)],
-    "mask2": [(0, 2)],
+    ("out", 0): [(8, 0)],
+    "ffn_out": [(0, 0), (8, 1)],
+    ("ffn", 0, 2): [(0, 1), (8, 2)],
+    ("ffn", 1, 0): [(8, 3)],
+    ("ffn", 1, 2): [(8, 4)],
+    ("in", 2): [(8, 5)],
+    "ffn_in": [(1, 0), (0, 2)],
+    ("cin", 0): [(8, 6)],
     "cross_in": [(1, 1)],
-    ("cross", 2, 0): [(0, 3)],
+    ("cross", 0, 0): [(8, 7)],
+    ("cross", 1, 0): [(0, 3)],
     "ck": [(2, 0)],
-    ("nrm", 2): [(1, 2), (2, 1)],
+    ("nrm", 0): [(1, 2)],
+    "norm": [(2, 1)],
     "self_out": [(3, 0), (0, 4)],
+    ("sin", 1): [(1, 3)],
     "self_in": [(3, 1)],
-    ("self", 0, 0): [(1, 3)],
-    ("self", 1, 0): [(2, 2)],
+    ("self", 0, 2): [(2, 2)],
     ("self", 1, 2): [(0, 5)],
-    ("self", 1, 3): [(3, 2)],
-    ("self", 2, 2): [(2, 3)],
-    ("self", 3, 0): [(1, 4)],
-    ("self", 3, 1): [(0, 6)],
-    ("self", 3, 2): [(3, 3)],
-    "qkv": [(4, 0), (5, 0)],
-    ("tok", 1): [(2, 4)],
-    ("tok", 2): [(4, 1), (5, 1)],
-    "end": [(0, 7), (1, 5), (0, 8), (4, 2), (3, 4), (5, 2), (1, 6), (6, 2), (2, 5), (7, 0), (4, 3), (5, 3), (3, 5), (1, 7), (7, 1), (6, 3), (4, 4), (2, 6), (5, 4), (1, 8), (3, 6), (4, 5), (7, 2), (6, 4), (2, 7), (5, 5), (2, 8), (7, 3), (3, 7), (4, 6), (3, 8), (7, 4), (5, 6), (4, 7), (7, 5), (5, 7), (4, 8), (5, 8), (7, 6), (7, 7)],
+    ("self", 2, 0): [(2, 3)],
+    ("self", 3, 0): [(1, 4), (0, 6)],
+    ("self", 3, 2): [(3, 2)],
+    ("qkv", 1): [(4, 0), (2, 4)],
+    "qkv": [(5, 0)],
+    ("tok", 1): [(4, 1)],
+    "tokens": [(5, 1), (6, 1)],
+    "end": [(0, 7), (7, 0), (3, 3), (0, 8), (4, 2), (2, 5), (5, 2), (6, 2), (7, 1), (4, 3), (1, 5), (5, 3), (7, 2), (2, 6), (3, 4), (6, 3), (1, 6), (4, 4), (5, 4), (2, 7), (2, 8), (7, 3), (3, 5), (6, 4), (1, 7), (7, 4), (4, 5), (5, 5), (3, 6), (7, 5), (5, 6), (7, 6), (4, 6), (3, 7), (7, 7), (5, 7), (3, 8), (1, 8), (4, 7), (5, 8), (4, 8)],
     "vectors": [(6, 0)],
-    "tokens": [(6, 1)],
 }
 
 
@@ -811,7 +819,7 @@
         in_specs=[WHOLE] * 6 + [ANY] * len(INS),
         out_specs=[ANY] * 4 + [WHOLE],
         scratch_shapes=[pltpu.VMEM(*x) for x in scratch]
-        + [pltpu.SemaphoreType.DMA((40,)), steps, steps] + [pltpu.SemaphoreType.DMA(((3 + PIECES) * seq,))] * 2,
+        + [pltpu.SemaphoreType.DMA((40,)), steps, steps] + [pltpu.SemaphoreType.DMA(((1 + 2 * PIECES) * seq,))] * 2,
         compiler_params=pltpu.CompilerParams(vmem_limit_bytes=62 * 2**20, collective_id=1, has_side_effects=True),
         name="main",
     )(tl, sl, *small, *[ins[name] for name in INS])

time: 209 us -> 209 us (level)
    pallas_call x1, Pallas kernels: 64.8 us -> 61.9 us  [forward(): pl.pallas_call(forward_kernel, out_shape=[jax.ShapeDtypeStruct(*o) for o...]
    pallas_call x1, Pallas kernels: 129 us -> 131 us  [main(): pl.pallas_call(functools.partial(main_kernel, PLAN), out_shape=[jax.Shape...]
where the time goes in v2:
time: 209 us; the launch traced here: 206 us
  Pallas kernels  204 us (98%)
    pallas_call x1, Pallas kernels, main(): pl.pallas_call(functools.partial(main_kernel, PLAN), out_shape=[jax.Shape...  131 us
    pallas_call x1, Pallas kernels, forward(): pl.pallas_call(forward_kernel, out_shape=[jax.ShapeDtypeStruct(*o) for o...  61.9 us
    pallas_call x1, Pallas kernels, unpack(): pl.pallas_call(unpack_kernel, out_shape=[jax.ShapeDtypeStruct(o, F32) for...  10.8 us

profile of v2, /device:TPU:0, one launch (start us, length us, event | category | flops | bytes accessed | tf_op | source)
XLA Modules:
  0.0 205.7 jit_solution(17264785061999169123)
XLA Ops:
  0.7 61.9 %forward.1 = (bf16[1024,512]{1,0:T(8,128)(2,1)}, bf16[1024,512]{1,0:T(8,128)(2,1)}, bf16[256,512]{1,0:T(8,128)(2,1)}, bf16[1024,512]{1,0:T(8,128)(2,1)}, bf16[51...) custom-call(bf16[4,256,512]{2,1,0:T(8,128)(2,1)} %tok_ref.1, ...), custom_call_target="tpu_custom_call" | custom-call | tf_op jit(solution)/shard_map/forward/pallas_call | solution.py:786
  62.6 131.1 %main.1 = (bf16[4,256,512]{2,1,0:T(8,128)(2,1)}, bf16[4,256,512]{2,1,0:T(8,128)(2,1)}, bf16[4,64,512]{2,1,0:T(8,128)(2,1)}, bf16[2,8192,256]{2,1,0:T(8,128)(2,1)}, f32[24,512]{1,0:T(8,128)}) custom-call(s32[4,32]{1,0:T(4,128)} %tl_ref.3, s32[4,32]{1,0:T(4,128)} %sl_ref.3, bf16[2048]{0:T(1024)(128)(2,1)} %bfi.1, bf16[512]{0:T(512)(128)(2,1)} %bfo.1, ...), custom_call_target="tpu_custom_call" | custom-call | tf_op jit(solution)/shard_map/main/pallas_call | solution.py:810
  193.6 0.0 copy-start
  193.7 10.8 %unpack.1 = (f32[512,1536]{1,0:T(8,128)}, f32[512,512]{1,0:T(8,128)}, f32[512,512]{1,0:T(8,128)}, f32[512,1024]{1,0:T(8,128)}, f32[512,512]{1,0:T(8,128)}, /*ind...) custom-call(bf16[2,8192,256]{2,1,0:T(8,128)(2,1)} %get-tuple-element, ...), custom_call_target="tpu_custom_call" | custom-call | tf_op jit(solution)/shard_map/unpack/pallas_call | solution.py:831
  204.5 0.0 copy-done
  204.5 1.0 copy.41
Async XLA Ops:
  193.6 10.8 %copy-start = (bf16[4,256,512]{2,1,0:T(8,128)(2,1)S(1)}, bf16[4,256,512]{2,1,0:T(8,128)(2,1)}, u32[]{:S(2)}) copy-start(bf16[4,256,512]{2,1,0:T(8,128)(2,1)} %get-tuple-element.128) | copy-start | bytes 3145732
